TPU v7x, 512 devices: a whole 4x8x8 slice. The times are simulated.
512 devices in a mesh: dp: 32 (over y, x), tensor: 16 (over z, core).
Axes of the slice: x: 4, y: 8, z: 8, core: 2. Of those that a mesh axis runs over, the one named last changes fastest.
Arguments:
- gate_pre: bfloat16 [8192, 28672], P('dp', 'tensor'), parts along dimension 0, may hold values from -6 to 6
- up_pre: bfloat16 [8192, 28672], P('dp', 'tensor'), parts along dimension 0, may hold values from -6 to 6
- signs: int32 [28672], P('tensor'), may hold values from -1 to 1, as said below
- hadamard: int32 [28, 28], replicated, may hold values from -1 to 1, as said below
- down_weight: bfloat16 [28672, 4096], P('tensor'), may hold values from -0.03125 to 0.03125
Outputs:
- mixed: bfloat16 [8192, 4096], P(('dp', 'tensor')), parts along dimension 0
There are 32 independent parts, one for each index of `dp`. A program takes and returns all parts, laid end to end along the dimension named above; an argument that names none is the same for every part. Nothing has to cross between parts.
Inputs may be any that keep to these rules, and one draw needn't show every extreme that they name: `signs`: every entry is -1 or 1. `hadamard`: a Hadamard matrix: entries -1 or 1, any two distinct rows orthogonal.
All inputs are finite; a program needn't handle non-finite values.
Results may differ from a plain program's by a relative error of at most 0.028.
Values may be sent and summed in bfloat16 or wider, within the bound.
No kernel may reach another device: no remote copies, remote signals or barrier semaphores. Data moves between devices by JAX's collectives and lax.ppermute only.
A program may use at most 64 MiB of HBM per device.

v0:
```python
import math

import jax
import jax.numpy as jnp
from jax import lax
from jax.sharding import PartitionSpec as P

FFN_UNITS = 28672


def partner_2(value, axis, bit):
    mask = 2**bit
    pairs = [(source, source ^ mask) for source in range(lax.axis_size(axis))]
    return lax.ppermute(value, axis, pairs)


def sylvester_matrix(order):
    position = jnp.arange(order, dtype=jnp.int32)
    common = position[:, None] & position[None, :]
    parity = jnp.zeros((order, order), dtype=jnp.int32)
    for bit_index in range(max(order.bit_length(), 1)):
        parity = parity + (common >> bit_index & 1)
    parity = parity % 2
    return (1 - 2 * parity).astype(jnp.float32)


def per_device(gate_pre, up_pre, signs, hadamard, down_weight):
    parts = lax.axis_size("tensor")
    tokens, width = gate_pre.shape
    local_order = width // 28
    scale = 1.0 / math.sqrt(FFN_UNITS)
    hidden = (
        jax.nn.silu(gate_pre.astype(jnp.float32))
        * up_pre.astype(jnp.float32)
        * signs.astype(jnp.float32)[None, :]
    )
    blocks = hidden.reshape(tokens, local_order, 28)
    inner = jnp.einsum(
        "tba,ae->tbe", blocks, hadamard.astype(jnp.float32), precision=lax.Precision.HIGHEST
    )
    inner = jnp.einsum(
        "tbe,bc->tce", inner, sylvester_matrix(local_order), precision=lax.Precision.HIGHEST
    )
    inner = inner.reshape(tokens, width)
    device = lax.axis_index("tensor")
    values = inner
    for level in range(parts.bit_length() - 1):
        partner = partner_2(values.astype(jnp.bfloat16), "tensor", level).astype(values.dtype)
        upper = device // (1 << level) % 2
        values = jnp.where(upper == 1, partner - values, values + partner)
    rotated = (values * scale).astype(jnp.bfloat16)
    return lax.psum_scatter(
        jnp.dot(rotated, down_weight, preferred_element_type=jnp.float32).astype(jnp.bfloat16),
        "tensor",
        scatter_dimension=0,
        tiled=True,
    )


def solution(mesh):
    placed = (P("dp", "tensor"), P("dp", "tensor"), P("tensor"), P(), P("tensor", None))
    return jax.shard_map(
        per_device, mesh=mesh, in_specs=placed, out_specs=P(("dp", "tensor"), None), check_vma=False
    )
```

profile of v0, /device:TPU:6, one launch (start us, length us, event | category | flops | bytes accessed | tf_op | source)
XLA Modules:
  0.0 234.5 jit_solution(7417738827033601761)
XLA Ops:
  6.5 0.0 reduce-scatter.2.cloned.1.call-start
  6.5 0.7 convert_element_type.48
  7.2 2.0 fusion.4
  9.2 1.7 copy.6
  11.0 0.0 copy-start.1
  11.0 1.6 reshape.7
  12.5 0.0 copy-done.1
  12.5 1.9 fusion.31
  14.4 2.7 %fusion.13 = f32[256,64,28]{0,1,2:T(8,128)S(1)} fusion(f32[256,64,28]{0,2,1:T(8,128)S(1)} %fusion.31), kind=kOutput, calls=%fused_computation.24 | convolution fusion | flops 352464896 | bytes 3670016 | tf_op jit(solution)/shard_map/tbe,bc->tce/dot_general | solution.py:41
  17.1 2.4 %copy.7 = f32[256,64,28]{0,2,1:T(8,128)} copy(f32[256,64,28]{0,1,2:T(8,128)S(1)} %fusion.13) | data formatting | bytes 3670016 | tf_op jit(solution)/shard_map/tbe,bc->tce/transpose | solution.py:41
  19.6 1.6 reshape.8
  21.2 1.0 convert_element_type.50
  22.2 1.9 collective-permute-start
  24.2 2.6 %collective-permute-done = bf16[256,1792]{0,1:T(8,128)(2,1)S(1)} collective-permute-done((bf16[256,1792]{0,1:T(8,128)(2,1)}, bf16[256,1792]{0,1:T(8,128)(2,1)S(1)}, u32[]{:S(2)}, u32[]{:S(2)}) %collective-permute-start) | collective-permute-done | bytes 917536 | tf_op jit(solution)/shard_map/ppermute | solution.py:14
  26.8 1.2 fusion.17
  28.0 4.3 %collective-permute-start.1 = (bf16[256,1792]{0,1:T(8,128)(2,1)}, bf16[256,1792]{0,1:T(8,128)(2,1)}, u32[]{:S(2)}, u32[]{:S(2)}) collective-permute-start(bf16[256,1792]{0,1:T(8,128)(2,1)} %fusion.17), channel_id=1, source_target_pairs={{0,2},{1,3},{2,0},{3,1},{4,6},{5,7},{6,4},{7,5},{8,10},{9,11},{10,... | collective-permute-start | bytes 2752520 | tf_op jit(solution)/shard_map/ppermute | solution.py:14
  32.3 20.9 %collective-permute-done.1 = bf16[256,1792]{0,1:T(8,128)(2,1)} collective-permute-done((bf16[256,1792]{0,1:T(8,128)(2,1)}, bf16[256,1792]{0,1:T(8,128)(2,1)}, u32[]{:S(2)}, u32[]{:S(2)}) %collective-permute-start.1) | collective-permute-done | bytes 917536 | tf_op jit(solution)/shard_map/ppermute | solution.py:14
  53.2 3.2 %fusion.49 = (bf16[256,1792]{0,1:T(8,128)(2,1)}, f32[256,1792]{0,1:T(8,128)}) fusion(f32[256,1792]{0,1:T(8,128)S(1)} %reshape.8, bf16[256,1792]{0,1:T(8,128)(2,1)S(1)} %collective-permute-done, pred[]{:T(512)S(6)} %eq.22, bf16[256,1792]{0,1:T(8,128)(2,1)} %collective-permute-done.1, pred[]{:T(512)S(6)} %eq.21), kind=kLoop, calls=%fused_computation.59 | loop fusion | flops 4128768 | bytes 6422530 | tf_op jit(solution)/shard_map/convert_element_type | solution.py:48
  56.4 6.1 %collective-permute-start.2 = (bf16[256,1792]{0,1:T(8,128)(2,1)}, bf16[256,1792]{0,1:T(8,128)(2,1)S(1)}, u32[]{:S(2)}, u32[]{:S(2)}) collective-permute-start(bf16[256,1792]{0,1:T(8,128)(2,1)} %get-tuple-element.5), channel_id=1, source_target_pairs={{0,4},{1,5},{2,6},{3,7},{4,0},{5,1},{6,2},{7,3},{8,12},{9,13},{10,... | collective-permute-start | bytes 2752520 | tf_op jit(solution)/shard_map/ppermute | solution.py:14
  62.6 40.0 %collective-permute-done.2 = bf16[256,1792]{0,1:T(8,128)(2,1)S(1)} collective-permute-done((bf16[256,1792]{0,1:T(8,128)(2,1)}, bf16[256,1792]{0,1:T(8,128)(2,1)S(1)}, u32[]{:S(2)}, u32[]{:S(2)}) %collective-permute-start.2) | collective-permute-done | bytes 917536 | tf_op jit(solution)/shard_map/ppermute | solution.py:14
  102.5 0.0 copy-start
  102.5 2.8 %fusion.16 = bf16[256,1792]{0,1:T(8,128)(2,1)} fusion(f32[256,1792]{0,1:T(8,128)} %get-tuple-element.6, bf16[256,1792]{0,1:T(8,128)(2,1)S(1)} %collective-permute-done.2, pred[]{:T(512)S(6)} %eq.20), kind=kLoop, calls=%fused_computation.25 | loop fusion | flops 2293760 | bytes 3670017 | tf_op jit(solution)/shard_map/convert_element_type | solution.py:48
  105.4 8.6 %collective-permute-start.3 = (bf16[256,1792]{0,1:T(8,128)(2,1)}, bf16[256,1792]{0,1:T(8,128)(2,1)}, u32[]{:S(2)}, u32[]{:S(2)}) collective-permute-start(bf16[256,1792]{0,1:T(8,128)(2,1)} %fusion.16), channel_id=1, source_target_pairs={{0,8},{1,9},{2,10},{3,11},{4,12},{5,13},{6,14},{7,15},{8,0},{9,1},... | collective-permute-start | bytes 2752520 | tf_op jit(solution)/shard_map/ppermute | solution.py:14
  114.0 39.7 %collective-permute-done.3 = bf16[256,1792]{0,1:T(8,128)(2,1)} collective-permute-done((bf16[256,1792]{0,1:T(8,128)(2,1)}, bf16[256,1792]{0,1:T(8,128)(2,1)}, u32[]{:S(2)}, u32[]{:S(2)}) %collective-permute-start.3) | collective-permute-done | bytes 917536 | tf_op jit(solution)/shard_map/ppermute | solution.py:14
  153.7 0.0 copy-done
  153.7 11.3 %convolution_convert_fusion = bf16[256,4096]{1,0:T(8,128)(2,1)} fusion(bf16[1792,4096]{1,0:T(8,128)(2,1)} %param.9, bf16[256,1792]{0,1:T(8,128)(2,1)} %collective-permute-done.3, f32[256,1792]{0,1:T(8,128)S(1)} %copy-done, bf16[256,1792]{0,1:T(8,128)(2,1)S(1)} %collective-permute-done.2, pred[]{:T(512)S(6)} %eq.20, pred[]{:T(512)S(6)} %eq.19), kind=kOutput, calls=%fused_computation | convolution fusion | flops 3763732480 | bytes 20447234 | tf_op jit(solution)/shard_map/dot_general | solution.py:53
  165.0 0.0 reduce-scatter.2.cloned.1.call-update
  165.1 62.6 %reduce-scatter.2.cloned.1.call-done = bf16[16,4096]{1,0:T(8,128)(2,1)} async-done(((bf16[256,4096]{1,0:T(8,128)(2,1)}), bf16[16,4096]{1,0:T(8,128)(2,1)}) %reduce-scatter.2.cloned.1.call-update) | async-done | bytes 131088 | tf_op jit(solution)/shard_map/reduce_scatter | solution.py:52
Async XLA Ops:
  6.5 221.1 %reduce-scatter.2.cloned.1.call-start = ((), (), s32[]{:S(2)}) async-start(), calls=%async_computation.1 | async-start | bytes 2228224 | tf_op jit(solution)/shard_map/reduce_scatter | solution.py:52
  11.0 1.6 copy-start.1
  22.2 4.6 %collective-permute-start = (bf16[256,1792]{0,1:T(8,128)(2,1)}, bf16[256,1792]{0,1:T(8,128)(2,1)S(1)}, u32[]{:S(2)}, u32[]{:S(2)}) collective-permute-start(bf16[256,1792]{0,1:T(8,128)(2,1)} %convert_element_type.50), channel_id=1, source_target_pairs={{0,1},{1,0},{2,3},{3,2},{4,5},{5,4},{6,7},{7,6},{8,9},{9,8},{10,11... | collective-permute-start | bytes 2752520 | tf_op jit(solution)/shard_map/ppermute | solution.py:14
  28.0 25.2 %collective-permute-start.1 = (bf16[256,1792]{0,1:T(8,128)(2,1)}, bf16[256,1792]{0,1:T(8,128)(2,1)}, u32[]{:S(2)}, u32[]{:S(2)}) collective-permute-start(bf16[256,1792]{0,1:T(8,128)(2,1)} %fusion.17), channel_id=1, source_target_pairs={{0,2},{1,3},{2,0},{3,1},{4,6},{5,7},{6,4},{7,5},{8,10},{9,11},{10,... | collective-permute-start | bytes 2752520 | tf_op jit(solution)/shard_map/ppermute | solution.py:14
  56.4 46.1 %collective-permute-start.2 = (bf16[256,1792]{0,1:T(8,128)(2,1)}, bf16[256,1792]{0,1:T(8,128)(2,1)S(1)}, u32[]{:S(2)}, u32[]{:S(2)}) collective-permute-start(bf16[256,1792]{0,1:T(8,128)(2,1)} %get-tuple-element.5), channel_id=1, source_target_pairs={{0,4},{1,5},{2,6},{3,7},{4,0},{5,1},{6,2},{7,3},{8,12},{9,13},{10,... | collective-permute-start | bytes 2752520 | tf_op jit(solution)/shard_map/ppermute | solution.py:14
  102.5 51.2 %copy-start = (f32[256,1792]{0,1:T(8,128)S(1)}, f32[256,1792]{0,1:T(8,128)}, u32[]{:S(2)}) copy-start(f32[256,1792]{0,1:T(8,128)} %get-tuple-element.6) | copy-start | bytes 5505028
  105.4 48.3 %collective-permute-start.3 = (bf16[256,1792]{0,1:T(8,128)(2,1)}, bf16[256,1792]{0,1:T(8,128)(2,1)}, u32[]{:S(2)}, u32[]{:S(2)}) collective-permute-start(bf16[256,1792]{0,1:T(8,128)(2,1)} %fusion.16), channel_id=1, source_target_pairs={{0,8},{1,9},{2,10},{3,11},{4,12},{5,13},{6,14},{7,15},{8,0},{9,1},... | collective-permute-start | bytes 2752520 | tf_op jit(solution)/shard_map/ppermute | solution.py:14
Sparse Core Ops, SparseCore 0:
  165.2 62.3 reduce-scatter.1
where the time goes:
time: 235 us; the launch traced here: 234 us
  waiting for transfers between devices  166 us (71%)
  starting transfers between devices  20.8 us (9%)
  matrix products  15.9 us (7%)
  between operations  13.6 us (6%)
  other arithmetic  11 us (5%)
  local copies, waits for them, and re-layouts  7.35 us (3%)
    ppermute x4, waiting for transfers between devices, partner_2(): return lax.ppermute(value, axis, pairs)  103 us
    reduce_scatter x1, waiting for transfers between devices, per_device(): lax.psum_scatter(jnp.dot(rotated, down_weight, preferred_element_type=jnp...  62.6 us
    ppermute x4, starting transfers between devices, partner_2(): return lax.ppermute(value, axis, pairs)  20.8 us
    dot_general x1, matrix products, per_device(): jnp.dot(rotated, down_weight, preferred_element_type=jnp.float32)  11.3 us
    convert_element_type x4, other arithmetic, per_device(): values.astype(jnp.bfloat16)  8.26 us
  transfers between devices with their start and end apart: 5, of which 5 were waited for; matrix products, arithmetic and copies ran while one was open for 0% of the time, Pallas kernels for 0%

commit v1 on v0

v1 whole, which is shorter than its diff:
```python
import math

import jax
import jax.numpy as jnp
import numpy as np
from jax import lax
from jax.experimental import pallas as pl
from jax.experimental.pallas import tpu as pltpu
from jax.sharding import PartitionSpec as P

FFN_UNITS = 28672
ORDER = 28
INNER = 32
SLAB = ORDER * INNER
LANES = 128


def sylvester(order):
    index = np.arange(order)
    common = index[:, None] & index[None, :]
    parity = np.zeros((order, order), np.int64)
    for bit in range(order.bit_length()):
        parity += common >> bit & 1
    return 1 - 2 * (parity % 2)


def slab_patterns():
    unit = np.arange(SLAB)
    outer = sylvester(INNER)[unit[:, None] // ORDER, unit[None, :] // ORDER]
    pick = (np.arange(INNER)[:, None] == unit[None, :] % ORDER)
    return outer, pick


def local_kernel(gate, up, signs, hadamard, outer, pick, pick_t, out, matrix):
    @pl.when(pl.program_id(0) == 0)
    def _():
        rows = jnp.dot(pick_t[...], hadamard[...], preferred_element_type=jnp.float32)
        spread = jnp.dot(
            rows.astype(jnp.bfloat16), pick[...], preferred_element_type=jnp.float32
        )
        matrix[...] = (spread * outer[...].astype(jnp.float32)).astype(jnp.bfloat16)

    half = 0.5 * gate[...].astype(jnp.float32)
    hidden = (half + half * jnp.tanh(half)) * (
        up[...].astype(jnp.float32) * signs[...].astype(jnp.float32)
    )
    out[...] = jnp.dot(
        hidden.astype(jnp.bfloat16), matrix[...], preferred_element_type=jnp.float32
    ).astype(jnp.bfloat16)


def local_transform(gate, up, signs, hadamard):
    tokens, width = gate.shape
    outer, pick = slab_patterns()
    padded = jnp.zeros((INNER, INNER), jnp.bfloat16).at[:ORDER, :ORDER].set(
        hadamard.astype(jnp.bfloat16)
    )
    whole = lambda shape: pl.BlockSpec(shape, lambda i: (0, 0))
    piece = pl.BlockSpec((tokens, SLAB), lambda i: (0, i))
    return pl.pallas_call(
        local_kernel,
        grid=(width // SLAB,),
        in_specs=[
            piece,
            piece,
            pl.BlockSpec((1, SLAB), lambda i: (0, i)),
            whole((INNER, INNER)),
            whole((SLAB, SLAB)),
            whole((INNER, SLAB)),
            whole((SLAB, INNER)),
        ],
        out_specs=piece,
        out_shape=jax.ShapeDtypeStruct((tokens, width), jnp.bfloat16),
        scratch_shapes=[pltpu.VMEM((SLAB, SLAB), jnp.bfloat16)],
        compiler_params=pltpu.CompilerParams(vmem_limit_bytes=24 << 20),
        name="local_transform",
    )(
        gate,
        up,
        signs.reshape(1, width),
        padded,
        jnp.asarray(outer, jnp.bfloat16),
        jnp.asarray(pick, jnp.bfloat16),
        jnp.asarray(pick.T, jnp.bfloat16),
    )


def across_kernel(scale, source, out):
    devices, tokens, width = source.shape
    slabs = width // SLAB
    for chunk in range(SLAB // LANES):
        values = []
        for device in range(devices):
            for slab in range(slabs):
                lanes = pl.ds(slab * SLAB + chunk * LANES, LANES)
                values.append(source[device, :, lanes].astype(jnp.float32))
        step = 1
        while step < len(values):
            for low in range(len(values)):
                if low & step == 0:
                    a, b = values[low], values[low | step]
                    values[low], values[low | step] = a + b, a - b
            step *= 2
        for index, value in enumerate(values):
            device, slab = divmod(index, slabs)
            lanes = pl.ds(slab * SLAB + chunk * LANES, LANES)
            out[device, :, lanes] = (value * scale).astype(jnp.bfloat16)


def across_transform(source):
    return pl.pallas_call(
        lambda source, out: across_kernel(1.0 / math.sqrt(FFN_UNITS), source, out),
        in_specs=[pl.BlockSpec(memory_space=pltpu.VMEM)],
        out_specs=pl.BlockSpec(memory_space=pltpu.VMEM),
        out_shape=jax.ShapeDtypeStruct(source.shape, jnp.bfloat16),
        compiler_params=pltpu.CompilerParams(vmem_limit_bytes=24 << 20),
        name="across_transform",
    )(source)


def per_device(gate_pre, up_pre, signs, hadamard, down_weight):
    parts = lax.axis_size("tensor")
    tokens, width = gate_pre.shape
    own = tokens // parts
    chips = parts // 2
    core = lax.axis_index("tensor") % 2
    inner = local_transform(gate_pre, up_pre, signs, hadamard)
    gathered = lax.all_to_all(inner.reshape(parts, own, width), "tensor", 0, 0)
    rotated = across_transform(gathered)
    back = lax.all_to_all(rotated, "tensor", 0, 0).reshape(chips, 2, own, width)

    def product(which):
        rows = lax.dynamic_index_in_dim(back, which, 1, keepdims=False)
        return jnp.dot(
            rows.reshape(chips * own, width), down_weight, preferred_element_type=jnp.float32
        ).astype(jnp.bfloat16)

    pairs = [(source, source ^ 1) for source in range(parts)]
    other = lax.ppermute(product(1 - core), "tensor", pairs)
    mine = product(core)
    both = (mine.astype(jnp.float32) + other.astype(jnp.float32)).astype(jnp.bfloat16)
    same_core = [[2 * chip + side for chip in range(chips)] for side in range(2)]
    terms = lax.all_to_all(
        both.reshape(chips, own, -1), "tensor", 0, 0, axis_index_groups=same_core
    )
    return jnp.sum(terms.astype(jnp.float32), axis=0).astype(jnp.bfloat16)


def solution(mesh):
    placed = (P("dp", "tensor"), P("dp", "tensor"), P("tensor"), P(), P("tensor", None))
    return jax.shard_map(
        per_device, mesh=mesh, in_specs=placed, out_specs=P(("dp", "tensor"), None), check_vma=False
    )
```

time: 235 us -> 128 us (0.54)
  waiting for transfers between devices: 166 us -> 25.7 us
  blocking collectives: 0 us -> 67.2 us
  between operations: 13.6 us -> 0.08 us
  starting transfers between devices: 20.8 us -> 7.91 us
  other arithmetic: 11 us -> 1.53 us
  Pallas kernels: 0 us -> 3.9 us
    ppermute x4 -> x1, waiting for transfers between devices: 103 us -> 2.26 us  [per_device(): other = lax.ppermute(product(1 - core), 'tensor', pairs)]
    all_to_all x0 -> x2, blocking collectives: none -> 67.2 us  [the longest x1 35.1 us: per_device(): gathered = lax.all_to_all(inner.reshape(parts, own, width), 'tensor', 0, 0)]
    reduce_scatter x1 -> x0, waiting for transfers between devices: 62.6 us -> none  [per_device(): lax.psum_scatter(jnp.dot(rotated, down_weight, preferred_element_type=jnp...]
    all_to_all x0 -> x1, waiting for transfers between devices: none -> 23.4 us  [per_device(): back = lax.all_to_all(rotated, 'tensor', 0, 0).reshape(chips, 2, own, width)]
    ppermute x4 -> x1, starting transfers between devices: 20.8 us -> 4.18 us  [per_device(): other = lax.ppermute(product(1 - core), 'tensor', pairs)]
    convert_element_type x5 -> x1, other arithmetic: 8.96 us -> 0.72 us  [local_transform(): hadamard.astype(jnp.bfloat16)]
    unnamed x4 -> x10, local copies, waits for them, and re-layouts: 0.01 us -> 5.53 us
    pallas_call x0 -> x2, Pallas kernels: none -> 3.9 us  [the longest x1 2.36 us: local_transform(): pl.pallas_call(local_kernel, grid=(width // SLAB,), in_specs=[piece, piec...]
  transfers between devices with their start and end apart: 5 -> 2, of which waited for: 5 -> 2; matrix products, arithmetic and copies ran while one was open for 0% -> 0% of each run, Pallas kernels for 0% -> 0%
where the time goes in v1:
time: 128 us; the launch traced here: 127 us
  blocking collectives  67.2 us (52%)
  waiting for transfers between devices  25.7 us (20%)
  matrix products  14.9 us (12%)
  starting transfers between devices  7.91 us (6%)
  local copies, waits for them, and re-layouts  6.3 us (5%)
  Pallas kernels  3.9 us (3%)
  other arithmetic  1.53 us (1%)
    all_to_all x1, blocking collectives, per_device(): gathered = lax.all_to_all(inner.reshape(parts, own, width), 'tensor', 0, 0)  35.1 us
    all_to_all x1, blocking collectives, per_device(): lax.all_to_all(both.reshape(chips, own, -1), 'tensor', 0, 0, axis_index_g...  32 us
    all_to_all x1, waiting for transfers between devices, per_device(): back = lax.all_to_all(rotated, 'tensor', 0, 0).reshape(chips, 2, own, width)  23.4 us
    dot_general x2, matrix products, product(): jnp.dot(rows.reshape(chips * own, width), down_weight, preferred_element_...  14.9 us
    unnamed x10, local copies, waits for them, and re-layouts  5.53 us
    ppermute x1, starting transfers between devices, per_device(): other = lax.ppermute(product(1 - core), 'tensor', pairs)  4.18 us
    all_to_all x1, starting transfers between devices, per_device(): back = lax.all_to_all(rotated, 'tensor', 0, 0).reshape(chips, 2, own, width)  3.73 us
  transfers between devices with their start and end apart: 2, of which 2 were waited for; matrix products, arithmetic and copies ran while one was open for 0% of the time, Pallas kernels for 0%

profile of v1, /device:TPU:6, one launch (start us, length us, event | category | flops | bytes accessed | tf_op | source)
XLA Modules:
  0.0 127.5 jit_solution(4688202601290252078)
XLA Ops:
  0.0 0.7 reshape.51.signs
  0.7 0.7 convert_element_type.20
  1.4 0.0 copy-start
  1.4 1.4 %copy-done = bf16[896,896]{1,0:T(8,128)(2,1)S(1)} copy-done((bf16[896,896]{1,0:T(8,128)(2,1)S(1)}, bf16[896,896]{1,0:T(8,128)(2,1)}, u32[]{:S(2)}) %copy-start) | copy-done | bytes 1605656
  2.9 0.0 copy-start.1
  2.9 1.2 copy-done.1
  4.0 0.0 copy-start.2
  4.0 1.2 copy-done.2
  5.2 0.0 copy-start.3
  5.2 0.9 copy-done.3
  6.2 0.0 copy-start.4
  6.2 0.8 copy-done.4
  7.0 2.4 %local_transform.1 = bf16[256,1792]{1,0:T(8,128)(2,1)S(1)} custom-call(bf16[256,1792]{1,0:T(8,128)(2,1)S(1)} %copy-done.1, bf16[256,1792]{1,0:T(8,128)(2,1)S(1)} %copy-done.2, s32[1,1792]{1,0:T(1,128)S(1)} %reshape.51.signs, bf16[32,32]{1,0:T(8,128)(2,1)S(1)} %scatter.4.hadamard, bf16[896,896]{1,0:T(8,128)(2,1)S(1)} %copy-done, ...), custom_call_target="tpu_custom_call" | custom-call | tf_op jit(solution)/shard_map/local_transform/pallas_call | solution.py:60
  9.3 35.1 %all_to_all.15.source = bf16[16,16,1792]{2,1,0:T(8,128)(2,1)S(1)} all-to-all(bf16[16,16,1792]{2,1,0:T(8,128)(2,1)S(1)} %bitcast.9), channel_id=1, replica_groups=mesh['dp'=32,'tensor'=16] {'tensor'}, dimensions={0} | all-to-all | bytes 1835008 | tf_op jit(solution)/shard_map/all_to_all | solution.py:128
  44.5 1.5 %across_transform.1 = bf16[16,16,1792]{2,1,0:T(8,128)(2,1)} custom-call(bf16[16,16,1792]{2,1,0:T(8,128)(2,1)S(1)} %all_to_all.15.source), custom_call_target="tpu_custom_call" | custom-call | tf_op jit(solution)/shard_map/across_transform/pallas_call | solution.py:111
  46.0 3.7 %all-to-all-start.1 = ((bf16[16,16,1792]{2,1,0:T(8,128)(2,1)}), bf16[16,16,1792]{2,1,0:T(8,128)(2,1)S(1)}, u32[]{:S(2)}, u32[]{:S(2)}) async-start(bf16[16,16,1792]{2,1,0:T(8,128)(2,1)} %across_transform.1), calls=%async_computation.1 | async-start | bytes 1835008 | tf_op jit(solution)/shard_map/all_to_all | solution.py:130
  49.8 23.4 %all-to-all-done.1 = bf16[16,16,1792]{2,1,0:T(8,128)(2,1)S(1)} async-done(((bf16[16,16,1792]{2,1,0:T(8,128)(2,1)}), bf16[16,16,1792]{2,1,0:T(8,128)(2,1)S(1)}, u32[]{:S(2)}, u32[]{:S(2)}) %all-to-all-start.1) | async-done | bytes 917536 | tf_op jit(solution)/shard_map/all_to_all | solution.py:130
  73.2 0.1 constant_dynamic-slice_fusion
  73.3 7.3 %convolution_convert_fusion = bf16[128,4096]{1,0:T(8,128)(2,1)S(1)} fusion(bf16[128,1792]{1,0:T(8,128)(2,1)S(1)} %bitcast.12, bf16[1792,4096]{1,0:T(8,128)(2,1)} %param.14), kind=kOutput, calls=%fused_computation | convolution fusion | flops 1879572480 | bytes 16187392 | tf_op jit(solution)/shard_map/dot_general | solution.py:134
  80.6 4.2 %collective-permute-start = (bf16[128,4096]{1,0:T(8,128)(2,1)S(1)}, bf16[128,4096]{1,0:T(8,128)(2,1)S(1)}, u32[]{:S(2)}, u32[]{:S(2)}) collective-permute-start(bf16[128,4096]{1,0:T(8,128)(2,1)S(1)} %convolution_convert_fusion), channel_id=1, source_target_pairs={{0,1},{1,0},{2,3},{3,2},{4,5},{5,4},{6,7},{7,6},{8,9},{9,8},{10,11... | collective-permute-start | bytes 3145736 | tf_op jit(solution)/shard_map/ppermute | solution.py:139
  84.8 2.3 %collective-permute-done = bf16[128,4096]{1,0:T(8,128)(2,1)S(1)} collective-permute-done((bf16[128,4096]{1,0:T(8,128)(2,1)S(1)}, bf16[128,4096]{1,0:T(8,128)(2,1)S(1)}, u32[]{:S(2)}, u32[]{:S(2)}) %collective-permute-start) | collective-permute-done | bytes 1048608 | tf_op jit(solution)/shard_map/ppermute | solution.py:139
  87.1 7.6 %add_convert_fusion = bf16[128,4096]{1,0:T(8,128)(2,1)S(1)} fusion(bf16[128,4096]{1,0:T(8,128)(2,1)S(1)} %collective-permute-done, bf16[128,1792]{1,0:T(8,128)(2,1)S(1)} %bitcast.13, bf16[1792,4096]{1,0:T(8,128)(2,1)} %param.14), kind=kOutput, calls=%fused_computation.3 | convolution fusion | flops 1881669632 | bytes 17235968 | tf_op jit(solution)/shard_map/dot_general | solution.py:134
  94.6 32.0 %all_to_all.16 = bf16[8,16,4096]{2,1,0:T(8,128)(2,1)S(1)} all-to-all(bf16[8,16,4096]{2,1,0:T(8,128)(2,1)S(1)} %bitcast.10), channel_id=1, replica_groups={{0,2,4,6,8,10,12,14},{1,3,5,7,9,11,13,15},{16,18,20,22,24,26,28,30},{17..., dimensions={0} | all-to-all | bytes 2097152 | tf_op jit(solution)/shard_map/all_to_all | solution.py:143
  126.7 0.8 reduce_sum.12
  (1 shorter events, 0.0 us)
Async XLA Ops:
  1.4 1.4 %copy-start = (bf16[896,896]{1,0:T(8,128)(2,1)S(1)}, bf16[896,896]{1,0:T(8,128)(2,1)}, u32[]{:S(2)}) copy-start(bf16[896,896]{1,0:T(8,128)(2,1)} %constant.62.clone.outer) | copy-start | bytes 4816900
  2.9 1.2 copy-start.1
  4.0 1.2 copy-start.2
  5.2 0.9 copy-start.3
  6.2 0.8 copy-start.4
  46.0 27.2 %all-to-all-start.1 = ((bf16[16,16,1792]{2,1,0:T(8,128)(2,1)}), bf16[16,16,1792]{2,1,0:T(8,128)(2,1)S(1)}, u32[]{:S(2)}, u32[]{:S(2)}) async-start(bf16[16,16,1792]{2,1,0:T(8,128)(2,1)} %across_transform.1), calls=%async_computation.1 | async-start | bytes 1835008 | tf_op jit(solution)/shard_map/all_to_all | solution.py:130
  80.6 6.5 %collective-permute-start = (bf16[128,4096]{1,0:T(8,128)(2,1)S(1)}, bf16[128,4096]{1,0:T(8,128)(2,1)S(1)}, u32[]{:S(2)}, u32[]{:S(2)}) collective-permute-start(bf16[128,4096]{1,0:T(8,128)(2,1)S(1)} %convolution_convert_fusion), channel_id=1, source_target_pairs={{0,1},{1,0},{2,3},{3,2},{4,5},{5,4},{6,7},{7,6},{8,9},{9,8},{10,11... | collective-permute-start | bytes 3145736 | tf_op jit(solution)/shard_map/ppermute | solution.py:139

commit v2 on v1

v2 whole, which is shorter than its diff:
```python
import math

import jax
import jax.numpy as jnp
from jax import lax
from jax.experimental import pallas as pl
from jax.experimental.pallas import tpu as pltpu
from jax.sharding import PartitionSpec as P

FFN_UNITS = 28672
ORDER = 28
INNER = 32
SLAB = ORDER * INNER
LANES = 128
COLUMNS = 512


def outer_index(unit):
    return (unit * 2341) >> 16


def iota(shape, dim):
    return lax.broadcasted_iota(jnp.int32, shape, dim)


def picks(condition):
    return jnp.where(condition, 1.0, 0.0).astype(jnp.bfloat16)


def slab_matrix(hadamard):
    tall, wide = (SLAB, INNER), (INNER, SLAB)
    tall_unit, wide_unit = iota(tall, 0), iota(wide, 1)
    tall_outer, wide_outer = outer_index(tall_unit), outer_index(wide_unit)
    pick_outer = picks(wide_outer == iota(wide, 0))
    pick_inner = picks(wide_unit - ORDER * wide_outer == iota(wide, 0))[:ORDER]
    tall_inner = picks(tall_unit - ORDER * tall_outer == iota(tall, 1))[:, :ORDER]
    common = tall_outer & iota(tall, 1)
    for shift in (4, 2, 1):
        common = common ^ (common >> shift)
    outer_rows = (1 - 2 * (common & 1)).astype(jnp.float32).astype(jnp.bfloat16)
    inner_rows = jnp.dot(
        tall_inner,
        hadamard.astype(jnp.float32).astype(jnp.bfloat16),
        preferred_element_type=jnp.float32,
    ).astype(jnp.bfloat16)
    inner = jnp.dot(inner_rows, pick_inner, preferred_element_type=jnp.float32)
    outer = jnp.dot(outer_rows, pick_outer, preferred_element_type=jnp.float32)
    return (inner * outer).astype(jnp.bfloat16)


def local_kernel(
    gate_hbm, up_hbm, signs_hbm, hadamard_hbm, out, gate, up, signs, hadamard, matrix, arrived, ready
):
    width = gate.shape[1]
    small = [
        pltpu.make_async_copy(source, held, ready.at[index])
        for index, (source, held) in enumerate(((hadamard_hbm, hadamard), (signs_hbm, signs)))
    ]
    for copy in small:
        copy.start()
    copies = []
    for slab in range(width // SLAB):
        lanes = pl.ds(slab * SLAB, SLAB)
        pair = [
            pltpu.make_async_copy(source.at[:, lanes], held.at[:, lanes], arrived.at[slab, index])
            for index, (source, held) in enumerate(((gate_hbm, gate), (up_hbm, up)))
        ]
        for copy in pair:
            copy.start()
        copies.append(pair)
    for copy in small:
        copy.wait()
    matrix[...] = slab_matrix(hadamard[...])
    for slab, pair in enumerate(copies):
        for copy in pair:
            copy.wait()
        lanes = pl.ds(slab * SLAB, SLAB)
        half = 0.5 * gate[:, lanes].astype(jnp.float32)
        sign = signs[lanes].astype(jnp.float32).reshape(1, SLAB)
        hidden = (half + half * jnp.tanh(half)) * (up[:, lanes].astype(jnp.float32) * sign)
        out[:, lanes] = jnp.dot(
            hidden.astype(jnp.bfloat16), matrix[...], preferred_element_type=jnp.float32
        ).astype(jnp.bfloat16)


def local_transform(gate, up, signs, hadamard):
    tokens, width = gate.shape
    vmem = pl.BlockSpec(memory_space=pltpu.VMEM)
    return pl.pallas_call(
        local_kernel,
        in_specs=[pl.BlockSpec(memory_space=pl.ANY)] * 4,
        out_specs=vmem,
        out_shape=jax.ShapeDtypeStruct((tokens, width), jnp.bfloat16),
        scratch_shapes=[
            pltpu.VMEM((tokens, width), jnp.bfloat16),
            pltpu.VMEM((tokens, width), jnp.bfloat16),
            pltpu.VMEM((width,), jnp.int32),
            pltpu.VMEM((ORDER, ORDER), jnp.int32),
            pltpu.VMEM((SLAB, SLAB), jnp.bfloat16),
            pltpu.SemaphoreType.DMA((width // SLAB, 2)),
            pltpu.SemaphoreType.DMA((2,)),
        ],
        compiler_params=pltpu.CompilerParams(vmem_limit_bytes=59 << 20),
        name="local_transform",
    )(gate, up, signs, hadamard)


def across_kernel(source, out):
    devices, tokens, width = source.shape
    slabs = width // SLAB
    core = lax.axis_index("tensor") % 2
    for chunk in range(SLAB // LANES):
        values = []
        for device in range(devices):
            for slab in range(slabs):
                lanes = pl.ds(slab * SLAB + chunk * LANES, LANES)
                values.append(source[device, :, lanes].astype(jnp.float32))
        step = 1
        while step < len(values):
            for low in range(len(values)):
                if low & step == 0:
                    a, b = values[low], values[low | step]
                    values[low], values[low | step] = a + b, a - b
            step *= 2
        for index, value in enumerate(values):
            device, slab = divmod(index, slabs)
            chip, side = divmod(device, 2)
            lanes = pl.ds(slab * SLAB + chunk * LANES, LANES)
            place = core if side == 0 else 1 - core
            out[chip, place, :, lanes] = (value * (1.0 / math.sqrt(FFN_UNITS))).astype(jnp.bfloat16)


def across_transform(source):
    devices, tokens, width = source.shape
    return pl.pallas_call(
        across_kernel,
        in_specs=[pl.BlockSpec(memory_space=pltpu.VMEM)],
        out_specs=pl.BlockSpec(memory_space=pltpu.VMEM),
        out_shape=jax.ShapeDtypeStruct((devices // 2, 2, tokens, width), jnp.bfloat16),
        compiler_params=pltpu.CompilerParams(vmem_limit_bytes=20 << 20),
        name="across_transform",
    )(source)


def product_kernel(rows, other, own_hbm, out, own, arrived):
    tiles = arrived.shape[0]
    chips, _, tokens, width = rows.shape
    lanes = lambda tile: pl.ds(pl.multiple_of(tile * COLUMNS, COLUMNS), COLUMNS)
    copy = lambda tile: pltpu.make_async_copy(
        own_hbm.at[:, lanes(tile)], own.at[:, lanes(tile)], arrived.at[tile]
    )
    for tile in range(tiles):
        copy(tile).start()

    @pl.loop(0, tiles)
    def _(tile):
        copy(tile).wait()
        total = other[:, lanes(tile)] + jnp.dot(
            rows[:, 0].reshape(chips * tokens, width),
            own[:, lanes(tile)],
            preferred_element_type=jnp.float32,
        )
        out[:, :, lanes(tile)] = total.astype(jnp.bfloat16).reshape(chips, tokens, COLUMNS)


def product(rows, other, own):
    chips, _, tokens, width = rows.shape
    columns = own.shape[1]
    vmem = pl.BlockSpec(memory_space=pltpu.VMEM)
    return pl.pallas_call(
        product_kernel,
        in_specs=[vmem, vmem, pl.BlockSpec(memory_space=pl.ANY)],
        out_specs=vmem,
        out_shape=jax.ShapeDtypeStruct((chips, tokens, columns), jnp.bfloat16),
        scratch_shapes=[
            pltpu.VMEM(own.shape, own.dtype),
            pltpu.SemaphoreType.DMA((columns // COLUMNS,)),
        ],
        compiler_params=pltpu.CompilerParams(vmem_limit_bytes=50 << 20),
        cost_estimate=pl.CostEstimate(
            flops=2 * chips * tokens * width * columns,
            transcendentals=0,
            bytes_accessed=own.size * own.dtype.itemsize,
        ),
        name="product",
    )(rows, other, own)


def per_device(gate_pre, up_pre, signs, hadamard, down_weight):
    parts = lax.axis_size("tensor")
    tokens, width = gate_pre.shape
    own = tokens // parts
    chips = parts // 2
    same_core = [[2 * chip + side for chip in range(chips)] for side in range(2)]
    pairs = [(source, source ^ 1) for source in range(parts)]
    inner = local_transform(gate_pre, up_pre, signs, hadamard)
    inner, down_weight = lax.optimization_barrier((inner, down_weight))
    other_weight = lax.ppermute(down_weight, "tensor", pairs)
    gathered = lax.all_to_all(inner.reshape(parts, own, width), "tensor", 0, 0)
    rotated = across_transform(gathered)
    back = lax.all_to_all(rotated, "tensor", 0, 0, axis_index_groups=same_core)
    sibling = jnp.dot(
        back[:, 1].reshape(chips * own, width), other_weight, preferred_element_type=jnp.float32
    )
    terms = product(back, sibling, down_weight)
    terms = lax.all_to_all(terms, "tensor", 0, 0, axis_index_groups=same_core)
    return jnp.sum(terms.astype(jnp.float32), axis=0).astype(jnp.bfloat16)


def solution(mesh):
    placed = (P("dp", "tensor"), P("dp", "tensor"), P("tensor"), P(), P("tensor", None))
    return jax.shard_map(
        per_device, mesh=mesh, in_specs=placed, out_specs=P(("dp", "tensor"), None), check_vma=False
    )
```

time: 128 us -> 115 us (0.90)
  blocking collectives: 67.2 us -> 97.1 us
  waiting for transfers between devices: 25.7 us -> 0.01 us
  matrix products: 14.9 us -> 2.07 us
  Pallas kernels: 3.9 us -> 11.5 us
  local copies, waits for them, and re-layouts: 6.3 us -> 0.03 us
  starting transfers between devices: 7.91 us -> 1.92 us
    all_to_all x1 -> x2, blocking collectives: 32 us -> 61.6 us  [the longest x1 31.6 us: per_device(): terms = lax.all_to_all(terms, 'tensor', 0, 0, axis_index_groups=same_core)]
    all_to_all x1 -> x0, waiting for transfers between devices: 23.4 us -> none  [per_device(): back = lax.all_to_all(rotated, 'tensor', 0, 0).reshape(chips, 2, own, width)]
    dot_general x2 -> x1, matrix products: 14.9 us -> 2.07 us  [per_device(): jnp.dot(back[:, 1].reshape(chips * own, width), other_weight, preferred_e...]
    pallas_call x2 -> x3, Pallas kernels: 3.9 us -> 11.5 us  [the longest x1 5.85 us: product(): pl.pallas_call(product_kernel, in_specs=[vmem, vmem, pl.BlockSpec(memory_...]
    unnamed x10 -> x0, local copies, waits for them, and re-layouts: 5.53 us -> none
    all_to_all x1 -> x0, starting transfers between devices: 3.73 us -> none  [per_device(): back = lax.all_to_all(rotated, 'tensor', 0, 0).reshape(chips, 2, own, width)]
    ppermute x1, waiting for transfers between devices: 2.26 us -> 0.01 us  [per_device(): other_weight = lax.ppermute(down_weight, 'tensor', pairs)]
    ppermute x1, starting transfers between devices: 4.18 us -> 1.92 us  [per_device(): other_weight = lax.ppermute(down_weight, 'tensor', pairs)]
  transfers between devices with their start and end apart: 2 -> 1, of which waited for: 2 -> 0; matrix products, arithmetic and copies ran while one was open for 0% -> 0% of each run, Pallas kernels for 0% -> 1%
where the time goes in v2:
time: 115 us; the launch traced here: 113 us
  blocking collectives  97.1 us (84%)
  Pallas kernels  11.5 us (10%)
  matrix products  2.07 us (2%)
  starting transfers between devices  1.92 us (2%)
    all_to_all x1, blocking collectives, per_device(): gathered = lax.all_to_all(inner.reshape(parts, own, width), 'tensor', 0, 0)  35.4 us
    all_to_all x1, blocking collectives, per_device(): terms = lax.all_to_all(terms, 'tensor', 0, 0, axis_index_groups=same_core)  31.6 us
    all_to_all x1, blocking collectives, per_device(): back = lax.all_to_all(rotated, 'tensor', 0, 0, axis_index_groups=same_core)  30 us
    pallas_call x1, Pallas kernels, product(): pl.pallas_call(product_kernel, in_specs=[vmem, vmem, pl.BlockSpec(memory_...  5.85 us
    pallas_call x1, Pallas kernels, local_transform(): pl.pallas_call(local_kernel, in_specs=[pl.BlockSpec(memory_space=pl.ANY)]...  4.95 us
  transfers between devices with their start and end apart: 1, of which 0 were waited for; matrix products, arithmetic and copies ran while one was open for 0% of the time, Pallas kernels for 1%

profile of v2, /device:TPU:6, one launch (start us, length us, event | category | flops | bytes accessed | tf_op | source)
XLA Modules:
  0.0 113.5 jit_solution(15715456206129719553)
XLA Ops:
  0.0 5.0 %local_transform.1 = bf16[256,1792]{1,0:T(8,128)(2,1)} custom-call(bf16[256,1792]{1,0:T(8,128)(2,1)} %gate_hbm.1, bf16[256,1792]{1,0:T(8,128)(2,1)} %up_hbm.1, s32[1792]{0:T(1024)} %signs_hbm.1, s32[28,28]{1,0:T(8,128)} %hadamard_hbm.1), custom_call_target="tpu_custom_call" | custom-call | tf_op jit(solution)/shard_map/local_transform/pallas_call | solution.py:89
  5.0 1.9 %collective-permute-start = (bf16[1792,4096]{1,0:T(8,128)(2,1)}, bf16[1792,4096]{1,0:T(8,128)(2,1)S(1)}, u32[]{:S(2)}, u32[]{:S(2)}) collective-permute-start(bf16[1792,4096]{1,0:T(8,128)(2,1)} %own_hbm), channel_id=1, source_target_pairs={{0,1},{1,0},{2,3},{3,2},{4,5},{5,4},{6,7},{7,6},{8,9},{9,8},{10,11... | collective-permute-start | bytes 44040200 | tf_op jit(solution)/shard_map/ppermute | solution.py:198
  6.9 35.4 %all_to_all.15.source = bf16[16,16,1792]{2,1,0:T(8,128)(2,1)S(1)} all-to-all(bf16[16,16,1792]{2,1,0:T(8,128)(2,1)} %bitcast.4), channel_id=1, replica_groups=mesh['dp'=32,'tensor'=16] {'tensor'}, dimensions={0} | all-to-all | bytes 1835008 | tf_op jit(solution)/shard_map/all_to_all | solution.py:199
  42.3 0.7 across_transform.1
  43.0 30.0 %all_to_all.16.rows = bf16[8,2,16,1792]{3,2,1,0:T(8,128)(2,1)S(1)} all-to-all(bf16[8,2,16,1792]{3,2,1,0:T(8,128)(2,1)S(1)} %across_transform.1), channel_id=1, replica_groups={{0,2,4,6,8,10,12,14},{1,3,5,7,9,11,13,15},{16,18,20,22,24,26,28,30},{17..., dimensions={0} | all-to-all | bytes 1835008 | tf_op jit(solution)/shard_map/all_to_all | solution.py:201
  73.1 0.0 collective-permute-done
  73.1 2.1 %fusion.other = f32[128,4096]{1,0:T(8,128)S(1)} fusion(bf16[128,1792]{1,0:T(8,128)(2,1)S(1)} %bitcast.5, bf16[1792,4096]{1,0:T(8,128)(2,1)S(1)} %collective-permute-done), kind=kOutput, calls=%fused_computation | convolution fusion | flops 1879048192 | bytes 17235968 | tf_op jit(solution)/shard_map/dot_general | solution.py:202
  75.2 5.9 %product.1 = bf16[8,16,4096]{2,1,0:T(8,128)(2,1)S(1)} custom-call(bf16[8,2,16,1792]{3,2,1,0:T(8,128)(2,1)S(1)} %all_to_all.16.rows, f32[128,4096]{1,0:T(8,128)S(1)} %fusion.other, bf16[1792,4096]{1,0:T(8,128)(2,1)} %own_hbm), custom_call_target="tpu_custom_call" | custom-call | flops 1879048192 | bytes 14680064 | tf_op jit(solution)/shard_map/product/pallas_call | solution.py:170
  81.0 31.6 %all_to_all.17 = bf16[8,16,4096]{2,1,0:T(8,128)(2,1)S(1)} all-to-all(bf16[8,16,4096]{2,1,0:T(8,128)(2,1)S(1)} %product.1), channel_id=1, replica_groups={{0,2,4,6,8,10,12,14},{1,3,5,7,9,11,13,15},{16,18,20,22,24,26,28,30},{17..., dimensions={0} | all-to-all | bytes 2097152 | tf_op jit(solution)/shard_map/all_to_all | solution.py:206
  112.7 0.8 reduce_sum.12
  (1 shorter events, 0.0 us)
Async XLA Ops:
  5.0 68.1 %collective-permute-start = (bf16[1792,4096]{1,0:T(8,128)(2,1)}, bf16[1792,4096]{1,0:T(8,128)(2,1)S(1)}, u32[]{:S(2)}, u32[]{:S(2)}) collective-permute-start(bf16[1792,4096]{1,0:T(8,128)(2,1)} %own_hbm), channel_id=1, source_target_pairs={{0,1},{1,0},{2,3},{3,2},{4,5},{5,4},{6,7},{7,6},{8,9},{9,8},{10,11... | collective-permute-start | bytes 44040200 | tf_op jit(solution)/shard_map/ppermute | solution.py:198

commit v3 on v2

--- a/solution.py
+++ b/solution.py
@@ -13,6 +13,7 @@
 SLAB = ORDER * INNER
 LANES = 128
 COLUMNS = 512
+KEPT = 15
 
 
 def outer_index(unit):
@@ -142,15 +143,23 @@
     )(source)
 
 
-def product_kernel(rows, other, own_hbm, out, own, arrived):
+def product_kernel(rows, other, own_hbm, out, own, spare, arrived):
     tiles = arrived.shape[0]
     chips, _, tokens, width = rows.shape
+    kept = chips * KEPT
     lanes = lambda tile: pl.ds(pl.multiple_of(tile * COLUMNS, COLUMNS), COLUMNS)
     copy = lambda tile: pltpu.make_async_copy(
         own_hbm.at[:, lanes(tile)], own.at[:, lanes(tile)], arrived.at[tile]
     )
     for tile in range(tiles):
         copy(tile).start()
+    square = (chips * tokens, chips * tokens)
+    target = iota(square, 0)
+    chip = (target * 4370) >> 16
+    origin = jnp.where(
+        target < kept, tokens * chip + target - KEPT * chip, tokens * (target - kept) + KEPT
+    )
+    order = picks(iota(square, 1) == origin)
 
     @pl.loop(0, tiles)
     def _(tile):
@@ -160,21 +169,32 @@
             own[:, lanes(tile)],
             preferred_element_type=jnp.float32,
         )
-        out[:, :, lanes(tile)] = total.astype(jnp.bfloat16).reshape(chips, tokens, COLUMNS)
+        ordered = jnp.dot(order, total.astype(jnp.bfloat16), preferred_element_type=jnp.float32)
+        out[:, lanes(tile)] = ordered[:kept].astype(jnp.bfloat16)
+        spare[pl.ds(pl.multiple_of(tile * chips, chips), chips), :] = ordered[kept:]
+
+    shape = (kept, tiles * chips)
+    piece, owner = iota(shape, 1) >> 3, iota(shape, 1) & 7
+    place = picks(iota(shape, 0) == KEPT * owner + piece)
+    out[:, tiles * COLUMNS :] = jnp.dot(
+        place, spare[...].astype(jnp.bfloat16), preferred_element_type=jnp.float32
+    ).astype(jnp.bfloat16)
 
 
 def product(rows, other, own):
     chips, _, tokens, width = rows.shape
     columns = own.shape[1]
+    tiles = columns // COLUMNS
     vmem = pl.BlockSpec(memory_space=pltpu.VMEM)
     return pl.pallas_call(
         product_kernel,
         in_specs=[vmem, vmem, pl.BlockSpec(memory_space=pl.ANY)],
         out_specs=vmem,
-        out_shape=jax.ShapeDtypeStruct((chips, tokens, columns), jnp.bfloat16),
+        out_shape=jax.ShapeDtypeStruct((chips * KEPT, columns + COLUMNS), jnp.bfloat16),
         scratch_shapes=[
             pltpu.VMEM(own.shape, own.dtype),
-            pltpu.SemaphoreType.DMA((columns // COLUMNS,)),
+            pltpu.VMEM((tiles * chips, COLUMNS), jnp.float32),
+            pltpu.SemaphoreType.DMA((tiles,)),
         ],
         compiler_params=pltpu.CompilerParams(vmem_limit_bytes=50 << 20),
         cost_estimate=pl.CostEstimate(
@@ -184,6 +204,31 @@
         ),
         name="product",
     )(rows, other, own)
+
+
+def unfold_kernel(source, out):
+    columns = out.shape[1]
+    shape = (out.shape[0], KEPT)
+    straight = picks(iota(shape, 0) == iota(shape, 1))
+    extra = source[:, columns:]
+    for piece in range(columns // COLUMNS):
+        lanes = pl.ds(piece * COLUMNS, COLUMNS)
+        last = picks((iota(shape, 0) == KEPT) & (iota(shape, 1) == piece))
+        out[:, lanes] = (
+            jnp.dot(straight, source[:, lanes], preferred_element_type=jnp.float32)
+            + jnp.dot(last, extra, preferred_element_type=jnp.float32)
+        ).astype(jnp.bfloat16)
+
+
+def unfold(source, tokens):
+    vmem = pl.BlockSpec(memory_space=pltpu.VMEM)
+    return pl.pallas_call(
+        unfold_kernel,
+        in_specs=[vmem],
+        out_specs=vmem,
+        out_shape=jax.ShapeDtypeStruct((tokens, source.shape[1] - COLUMNS), jnp.bfloat16),
+        name="unfold",
+    )(source)
 
 
 def per_device(gate_pre, up_pre, signs, hadamard, down_weight):
@@ -203,8 +248,10 @@
         back[:, 1].reshape(chips * own, width), other_weight, preferred_element_type=jnp.float32
     )
     terms = product(back, sibling, down_weight)
-    terms = lax.all_to_all(terms, "tensor", 0, 0, axis_index_groups=same_core)
-    return jnp.sum(terms.astype(jnp.float32), axis=0).astype(jnp.bfloat16)
+    total = lax.psum_scatter(
+        terms, "tensor", scatter_dimension=0, axis_index_groups=same_core, tiled=True
+    )
+    return unfold(total, own)
 
 
 def solution(mesh):

time: 115 us -> 111 us (0.965); the launches traced: 113 us -> 111 us
  blocking collectives: 97.1 us -> 86.2 us
  starting transfers between devices: 1.92 us -> 5.79 us
  local copies, waits for them, and re-layouts: 0.03 us -> 2.42 us
  Pallas kernels: 11.5 us -> 13.8 us
    all_to_all x1 -> x0, blocking collectives: 31.6 us -> none  [per_device(): terms = lax.all_to_all(terms, 'tensor', 0, 0, axis_index_groups=same_core)]
    unnamed x0 -> x1, blocking collectives: none -> 20.7 us
    unnamed x0 -> x1, starting transfers between devices: none -> 3.87 us
    unnamed x0 -> x4, local copies, waits for them, and re-layouts: none -> 2.39 us
    pallas_call x0 -> x1, Pallas kernels: none -> 1.77 us  [unfold(): pl.pallas_call(unfold_kernel, in_specs=[vmem], out_specs=vmem, out_shape=...]
  transfers between devices with their start and end apart: 1 -> 2, of which waited for: 0 -> 0; matrix products, arithmetic and copies ran while one was open for 0% -> 1% of each run, Pallas kernels for 1% -> 1%
where the time goes in v3:
time: 111 us
  blocking collectives  86.2 us (78%)
  Pallas kernels  13.8 us (12%)
  starting transfers between devices  5.79 us (5%)
  local copies, waits for them, and re-layouts  2.42 us (2%)
  matrix products  2.07 us (2%)
    all_to_all x1, blocking collectives, per_device(): gathered = lax.all_to_all(inner.reshape(parts, own, width), 'tensor', 0, 0)  35.4 us
    all_to_all x1, blocking collectives, per_device(): back = lax.all_to_all(rotated, 'tensor', 0, 0, axis_index_groups=same_core)  30 us
    unnamed x1, blocking collectives  20.7 us
    pallas_call x1, Pallas kernels, product(): pl.pallas_call(product_kernel, in_specs=[vmem, vmem, pl.BlockSpec(memory_...  6.38 us
    pallas_call x1, Pallas kernels, local_transform(): pl.pallas_call(local_kernel, in_specs=[pl.BlockSpec(memory_space=pl.ANY)]...  4.95 us
    unnamed x1, starting transfers between devices  3.87 us
    unnamed x4, local copies, waits for them, and re-layouts  2.39 us
  transfers between devices with their start and end apart: 2, of which 0 were waited for; matrix products, arithmetic and copies ran while one was open for 1% of the time, Pallas kernels for 1%

profile of v3, /device:TPU:6, one launch (start us, length us, event | category | flops | bytes accessed | tf_op | source)
XLA Modules:
  0.0 111.0 jit_solution(15674741137975117432)
XLA Ops:
  0.0 5.0 %local_transform.1 = bf16[256,1792]{1,0:T(8,128)(2,1)} custom-call(bf16[256,1792]{1,0:T(8,128)(2,1)} %gate_hbm.1, bf16[256,1792]{1,0:T(8,128)(2,1)} %up_hbm.1, s32[1792]{0:T(1024)} %signs_hbm.1, s32[28,28]{1,0:T(8,128)} %hadamard_hbm.1), custom_call_target="tpu_custom_call" | custom-call | tf_op jit(solution)/shard_map/local_transform/pallas_call | solution.py:90
  5.0 1.9 %collective-permute-start = (bf16[1792,4096]{1,0:T(8,128)(2,1)}, bf16[1792,4096]{1,0:T(8,128)(2,1)S(1)}, u32[]{:S(2)}, u32[]{:S(2)}) collective-permute-start(bf16[1792,4096]{1,0:T(8,128)(2,1)} %own_hbm), channel_id=1, source_target_pairs={{0,1},{1,0},{2,3},{3,2},{4,5},{5,4},{6,7},{7,6},{8,9},{9,8},{10,11... | collective-permute-start | bytes 44040200 | tf_op jit(solution)/shard_map/ppermute | solution.py:243
  6.9 35.4 %all_to_all.10.source = bf16[16,16,1792]{2,1,0:T(8,128)(2,1)S(1)} all-to-all(bf16[16,16,1792]{2,1,0:T(8,128)(2,1)} %bitcast.7), channel_id=1, replica_groups=mesh['dp'=32,'tensor'=16] {'tensor'}, dimensions={0} | all-to-all | bytes 1835008 | tf_op jit(solution)/shard_map/all_to_all | solution.py:244
  42.3 0.7 across_transform.1
  43.0 30.0 %all_to_all.11.rows = bf16[8,2,16,1792]{3,2,1,0:T(8,128)(2,1)S(1)} all-to-all(bf16[8,2,16,1792]{3,2,1,0:T(8,128)(2,1)S(1)} %across_transform.1), channel_id=1, replica_groups={{0,2,4,6,8,10,12,14},{1,3,5,7,9,11,13,15},{16,18,20,22,24,26,28,30},{17..., dimensions={0} | all-to-all | bytes 1835008 | tf_op jit(solution)/shard_map/all_to_all | solution.py:246
  73.1 0.0 collective-permute-done
  73.1 2.1 %fusion.1.other = f32[128,4096]{1,0:T(8,128)S(1)} fusion(bf16[128,1792]{1,0:T(8,128)(2,1)S(1)} %bitcast.8, bf16[1792,4096]{1,0:T(8,128)(2,1)S(1)} %collective-permute-done), kind=kOutput, calls=%fused_computation.1 | convolution fusion | flops 1879048192 | bytes 17235968 | tf_op jit(solution)/shard_map/dot_general | solution.py:247
  75.2 6.4 %product.1 = bf16[120,4608]{1,0:T(8,128)(2,1)S(1)} custom-call(bf16[8,2,16,1792]{3,2,1,0:T(8,128)(2,1)S(1)} %all_to_all.11.rows, f32[128,4096]{1,0:T(8,128)S(1)} %fusion.1.other, bf16[1792,4096]{1,0:T(8,128)(2,1)} %own_hbm), custom_call_target="tpu_custom_call" | custom-call | flops 1879048192 | bytes 14680064 | tf_op jit(solution)/shard_map/product/pallas_call | solution.py:189
  81.6 20.7 %fusion = bf16[16,4608]{1,0:T(8,128)(2,1)S(1)} fusion(bf16[120,4608]{1,0:T(8,128)(2,1)S(1)} %product.1), kind=kCustom, calls=%all-reduce-scatter | all-reduce-scatter fusion | flops 589825 | bytes 1255424
  102.3 3.9 %collective-permute-start.1 = (bf16[7,4608]{1,0:T(8,128)(2,1)S(1)}, bf16[7,4608]{1,0:T(8,128)(2,1)S(1)}, u32[]{:S(2)}, u32[]{:S(2)}) collective-permute-start(bf16[7,4608]{1,0:T(8,128)(2,1)S(1)} %slice.5), channel_id=1, source_target_pairs={{0,2},{2,4},{4,6},{6,8},{8,10},{10,12},{12,14},{1,3},{3,5},{5,7},{... | collective-permute-start | bytes 193544
  106.2 1.3 %dynamic-slice.4 = u32[1]{0:T(128)} dynamic-slice(u32[512]{0:T(512)} %constant.2, u32[]{:S(6)} %partition-id.4), dynamic_slice_sizes={1} | dynamic-slice | bytes 12
  108.1 0.0 collective-permute-done.1
  108.1 0.4 concatenate
  108.5 0.7 constant_dynamic-slice_fusion.source
  109.2 1.8 %unfold.1 = bf16[16,4096]{1,0:T(8,128)(2,1)} custom-call(bf16[15,4608]{1,0:T(8,128)(2,1)} %constant_dynamic-slice_fusion.source), custom_call_target="tpu_custom_call" | custom-call | tf_op jit(solution)/shard_map/unfold/pallas_call | solution.py:225
  (2 shorter events, 0.1 us)
Async XLA Ops:
  5.0 68.1 %collective-permute-start = (bf16[1792,4096]{1,0:T(8,128)(2,1)}, bf16[1792,4096]{1,0:T(8,128)(2,1)S(1)}, u32[]{:S(2)}, u32[]{:S(2)}) collective-permute-start(bf16[1792,4096]{1,0:T(8,128)(2,1)} %own_hbm), channel_id=1, source_target_pairs={{0,1},{1,0},{2,3},{3,2},{4,5},{5,4},{6,7},{7,6},{8,9},{9,8},{10,11... | collective-permute-start | bytes 44040200 | tf_op jit(solution)/shard_map/ppermute | solution.py:243
  102.3 5.8 %collective-permute-start.1 = (bf16[7,4608]{1,0:T(8,128)(2,1)S(1)}, bf16[7,4608]{1,0:T(8,128)(2,1)S(1)}, u32[]{:S(2)}, u32[]{:S(2)}) collective-permute-start(bf16[7,4608]{1,0:T(8,128)(2,1)S(1)} %slice.5), channel_id=1, source_target_pairs={{0,2},{2,4},{4,6},{6,8},{8,10},{10,12},{12,14},{1,3},{3,5},{5,7},{... | collective-permute-start | bytes 193544

commit v4 on v3

--- a/solution.py
+++ b/solution.py
@@ -13,6 +13,7 @@
 SLAB = ORDER * INNER
 LANES = 128
 COLUMNS = 512
+TILE = 512
 KEPT = 15
 
 
@@ -101,9 +102,9 @@
             pltpu.SemaphoreType.DMA((width // SLAB, 2)),
             pltpu.SemaphoreType.DMA((2,)),
         ],
-        compiler_params=pltpu.CompilerParams(vmem_limit_bytes=59 << 20),
+        compiler_params=pltpu.CompilerParams(vmem_limit_bytes=20 << 20),
         name="local_transform",
-    )(gate, up, signs, hadamard)
+    )(*(pltpu.with_memory_space_constraint(x, pltpu.HBM) for x in (gate, up, signs, hadamard)))
 
 
 def across_kernel(source, out):
@@ -143,16 +144,12 @@
     )(source)
 
 
-def product_kernel(rows, other, own_hbm, out, own, spare, arrived):
-    tiles = arrived.shape[0]
+def product_kernel(rows, other, own, out, ordered, spare):
+    tiles = own.shape[1] // TILE
     chips, _, tokens, width = rows.shape
     kept = chips * KEPT
-    lanes = lambda tile: pl.ds(pl.multiple_of(tile * COLUMNS, COLUMNS), COLUMNS)
-    copy = lambda tile: pltpu.make_async_copy(
-        own_hbm.at[:, lanes(tile)], own.at[:, lanes(tile)], arrived.at[tile]
-    )
-    for tile in range(tiles):
-        copy(tile).start()
+    columns = own.shape[1]
+    lanes = lambda tile: pl.ds(pl.multiple_of(tile * TILE, TILE), TILE)
     square = (chips * tokens, chips * tokens)
     target = iota(square, 0)
     chip = (target * 4370) >> 16
@@ -160,50 +157,54 @@
         target < kept, tokens * chip + target - KEPT * chip, tokens * (target - kept) + KEPT
     )
     order = picks(iota(square, 1) == origin)
-
-    @pl.loop(0, tiles)
-    def _(tile):
-        copy(tile).wait()
-        total = other[:, lanes(tile)] + jnp.dot(
-            rows[:, 0].reshape(chips * tokens, width),
-            own[:, lanes(tile)],
+    for place in (1, 0):
+        ordered[place] = jnp.dot(
+            order, rows[:, place].reshape(chips * tokens, width), preferred_element_type=jnp.float32
+        ).astype(jnp.bfloat16)
+
+    for tile in range(tiles):
+        total = jnp.dot(ordered[1], other[:, lanes(tile)], preferred_element_type=jnp.float32)
+        total += jnp.dot(ordered[0], own[:, lanes(tile)], preferred_element_type=jnp.float32)
+        out[:, lanes(tile)] = total[:kept].astype(jnp.bfloat16)
+        spare[:, lanes(tile)] = total[kept:].astype(jnp.bfloat16)
+
+    shape = (kept, chips)
+    row, owner = iota(shape, 0), iota(shape, 1)
+    extra = jnp.zeros((kept, COLUMNS), jnp.float32)
+    for piece in range(columns // COLUMNS):
+        extra += jnp.dot(
+            picks(row == KEPT * owner + piece),
+            spare[:, pl.ds(piece * COLUMNS, COLUMNS)],
             preferred_element_type=jnp.float32,
         )
-        ordered = jnp.dot(order, total.astype(jnp.bfloat16), preferred_element_type=jnp.float32)
-        out[:, lanes(tile)] = ordered[:kept].astype(jnp.bfloat16)
-        spare[pl.ds(pl.multiple_of(tile * chips, chips), chips), :] = ordered[kept:]
-
-    shape = (kept, tiles * chips)
-    piece, owner = iota(shape, 1) >> 3, iota(shape, 1) & 7
-    place = picks(iota(shape, 0) == KEPT * owner + piece)
-    out[:, tiles * COLUMNS :] = jnp.dot(
-        place, spare[...].astype(jnp.bfloat16), preferred_element_type=jnp.float32
-    ).astype(jnp.bfloat16)
+    out[:, columns:] = extra.astype(jnp.bfloat16)
 
 
 def product(rows, other, own):
     chips, _, tokens, width = rows.shape
     columns = own.shape[1]
-    tiles = columns // COLUMNS
     vmem = pl.BlockSpec(memory_space=pltpu.VMEM)
     return pl.pallas_call(
         product_kernel,
-        in_specs=[vmem, vmem, pl.BlockSpec(memory_space=pl.ANY)],
+        in_specs=[vmem, vmem, vmem],
         out_specs=vmem,
         out_shape=jax.ShapeDtypeStruct((chips * KEPT, columns + COLUMNS), jnp.bfloat16),
         scratch_shapes=[
-            pltpu.VMEM(own.shape, own.dtype),
-            pltpu.VMEM((tiles * chips, COLUMNS), jnp.float32),
-            pltpu.SemaphoreType.DMA((tiles,)),
+            pltpu.VMEM((2, chips * tokens, width), jnp.bfloat16),
+            pltpu.VMEM((chips, columns), jnp.bfloat16),
         ],
-        compiler_params=pltpu.CompilerParams(vmem_limit_bytes=50 << 20),
+        compiler_params=pltpu.CompilerParams(vmem_limit_bytes=16 << 20),
         cost_estimate=pl.CostEstimate(
-            flops=2 * chips * tokens * width * columns,
+            flops=4 * chips * tokens * width * columns,
             transcendentals=0,
             bytes_accessed=own.size * own.dtype.itemsize,
         ),
         name="product",
-    )(rows, other, own)
+    )(
+        rows,
+        pltpu.with_memory_space_constraint(other, pltpu.VMEM),
+        pltpu.with_memory_space_constraint(own, pltpu.VMEM),
+    )
 
 
 def unfold_kernel(source, out):
@@ -243,11 +244,10 @@
     other_weight = lax.ppermute(down_weight, "tensor", pairs)
     gathered = lax.all_to_all(inner.reshape(parts, own, width), "tensor", 0, 0)
     rotated = across_transform(gathered)
+    rotated, other_weight = lax.optimization_barrier((rotated, other_weight))
+    own_weight = lax.ppermute(other_weight, "tensor", pairs)
     back = lax.all_to_all(rotated, "tensor", 0, 0, axis_index_groups=same_core)
-    sibling = jnp.dot(
-        back[:, 1].reshape(chips * own, width), other_weight, preferred_element_type=jnp.float32
-    )
-    terms = product(back, sibling, down_weight)
+    terms = product(back, other_weight, own_weight)
     total = lax.psum_scatter(
         terms, "tensor", scatter_dimension=0, axis_index_groups=same_core, tiled=True
     )

time: 111 us -> 108 us (0.973)
  Pallas kernels: 13.8 us -> 10.9 us
  starting transfers between devices: 5.79 us -> 8.2 us
  matrix products: 2.07 us -> 0 us
    ppermute x0 -> x1, starting transfers between devices: none -> 3.16 us  [per_device(): own_weight = lax.ppermute(other_weight, 'tensor', pairs)]
    dot_general x1 -> x0, matrix products: 2.07 us -> none  [per_device(): jnp.dot(back[:, 1].reshape(chips * own, width), other_weight, preferred_e...]
    pallas_call x1, Pallas kernels: 6.38 us -> 4.46 us  [product(): pl.pallas_call(product_kernel, in_specs=[vmem, vmem, vmem], out_specs=vme...]
    all_to_all x1, blocking collectives: 30 us -> 28.8 us  [per_device(): back = lax.all_to_all(rotated, 'tensor', 0, 0, axis_index_groups=same_core)]
  transfers between devices with their start and end apart: 2 -> 3, of which waited for: 0 -> 0; matrix products, arithmetic and copies ran while one was open for 1% -> 1% of each run, Pallas kernels for 1% -> 1%
where the time goes in v4:
time: 108 us
  blocking collectives  85.4 us (79%)
  Pallas kernels  10.9 us (10%)
  starting transfers between devices  8.2 us (8%)
  local copies, waits for them, and re-layouts  2.39 us (2%)
    all_to_all x1, blocking collectives, per_device(): gathered = lax.all_to_all(inner.reshape(parts, own, width), 'tensor', 0, 0)  35.2 us
    all_to_all x1, blocking collectives, per_device(): back = lax.all_to_all(rotated, 'tensor', 0, 0, axis_index_groups=same_core)  28.8 us
    unnamed x1, blocking collectives  21.4 us
    pallas_call x1, Pallas kernels, product(): pl.pallas_call(product_kernel, in_specs=[vmem, vmem, vmem], out_specs=vme...  4.46 us
    pallas_call x1, Pallas kernels, local_transform(): pl.pallas_call(local_kernel, in_specs=[pl.BlockSpec(memory_space=pl.ANY)]...  4.03 us
    ppermute x1, starting transfers between devices, per_device(): own_weight = lax.ppermute(other_weight, 'tensor', pairs)  3.16 us
    unnamed x1, starting transfers between devices  3.12 us
    unnamed x4, local copies, waits for them, and re-layouts  2.39 us
  transfers between devices with their start and end apart: 3, of which 0 were waited for; matrix products, arithmetic and copies ran while one was open for 1% of the time, Pallas kernels for 1%

profile of v4, /device:TPU:6, one launch (start us, length us, event | category | flops | bytes accessed | tf_op | source)
XLA Modules:
  0.0 107.7 jit_solution(6916912725575046659)
XLA Ops:
  0.0 4.0 %local_transform.1 = bf16[256,1792]{1,0:T(8,128)(2,1)S(1)} custom-call(bf16[256,1792]{1,0:T(8,128)(2,1)} %gate_hbm.1, bf16[256,1792]{1,0:T(8,128)(2,1)} %up_hbm.1, s32[1792]{0:T(1024)} %signs_hbm.1, s32[28,28]{1,0:T(8,128)} %hadamard_hbm.1), custom_call_target="tpu_custom_call" | custom-call | tf_op jit(solution)/shard_map/local_transform/pallas_call | solution.py:91
  4.0 1.9 %collective-permute-start = (bf16[1792,4096]{1,0:T(8,128)(2,1)}, bf16[1792,4096]{1,0:T(8,128)(2,1)S(1)}, u32[]{:S(2)}, u32[]{:S(2)}) collective-permute-start(bf16[1792,4096]{1,0:T(8,128)(2,1)} %param.9), channel_id=1, source_target_pairs={{0,1},{1,0},{2,3},{3,2},{4,5},{5,4},{6,7},{7,6},{8,9},{9,8},{10,11... | collective-permute-start | bytes 44040200 | tf_op jit(solution)/shard_map/ppermute | solution.py:244
  6.0 35.2 %all_to_all.10.source = bf16[16,16,1792]{2,1,0:T(8,128)(2,1)S(1)} all-to-all(bf16[16,16,1792]{2,1,0:T(8,128)(2,1)S(1)} %bitcast.4), channel_id=1, replica_groups=mesh['dp'=32,'tensor'=16] {'tensor'}, dimensions={0} | all-to-all | bytes 1835008 | tf_op jit(solution)/shard_map/all_to_all | solution.py:245
  41.2 0.7 across_transform.1
  41.9 0.0 collective-permute-done.other
  41.9 3.2 %collective-permute-start.1 = (bf16[1792,4096]{1,0:T(8,128)(2,1)S(1)}, bf16[1792,4096]{1,0:T(8,128)(2,1)S(1)}, u32[]{:S(2)}, u32[]{:S(2)}) collective-permute-start(bf16[1792,4096]{1,0:T(8,128)(2,1)S(1)} %collective-permute-done.other), channel_id=1, source_target_pairs={{0,1},{1,0},{2,3},{3,2},{4,5},{5,4},{6,7},{7,6},{8,9},{9,8},{10,11... | collective-permute-start | bytes 44040200 | tf_op jit(solution)/shard_map/ppermute | solution.py:248
  45.1 28.8 %all_to_all.11.rows = bf16[8,2,16,1792]{3,2,1,0:T(8,128)(2,1)S(1)} all-to-all(bf16[8,2,16,1792]{3,2,1,0:T(8,128)(2,1)S(1)} %across_transform.1), channel_id=1, replica_groups={{0,2,4,6,8,10,12,14},{1,3,5,7,9,11,13,15},{16,18,20,22,24,26,28,30},{17..., dimensions={0} | all-to-all | bytes 1835008 | tf_op jit(solution)/shard_map/all_to_all | solution.py:249
  73.8 0.0 collective-permute-done.1.own
  73.8 4.5 %product.1 = bf16[120,4608]{1,0:T(8,128)(2,1)S(1)} custom-call(bf16[8,2,16,1792]{3,2,1,0:T(8,128)(2,1)S(1)} %all_to_all.11.rows, bf16[1792,4096]{1,0:T(8,128)(2,1)S(1)} %collective-permute-done.other, bf16[1792,4096]{1,0:T(8,128)(2,1)S(1)} %collective-permute-done.1.own), custom_call_target="tpu_custom_call" | custom-call | flops 3758096384 | bytes 14680064 | tf_op jit(solution)/shard_map/product/pallas_call | solution.py:187
  78.3 21.4 %fusion = bf16[16,4608]{1,0:T(8,128)(2,1)S(1)} fusion(bf16[120,4608]{1,0:T(8,128)(2,1)S(1)} %product.1), kind=kCustom, calls=%all-reduce-scatter | all-reduce-scatter fusion | flops 589825 | bytes 1255424
  99.8 3.1 %collective-permute-start.2 = (bf16[7,4608]{1,0:T(8,128)(2,1)S(1)}, bf16[7,4608]{1,0:T(8,128)(2,1)S(1)}, u32[]{:S(2)}, u32[]{:S(2)}) collective-permute-start(bf16[7,4608]{1,0:T(8,128)(2,1)S(1)} %slice), channel_id=1, source_target_pairs={{0,2},{2,4},{4,6},{6,8},{8,10},{10,12},{12,14},{1,3},{3,5},{5,7},{... | collective-permute-start | bytes 193544
  102.9 1.3 %dynamic-slice.4 = u32[1]{0:T(128)} dynamic-slice(u32[512]{0:T(512)} %constant.2, u32[]{:S(6)} %partition-id.4), dynamic_slice_sizes={1} | dynamic-slice | bytes 12
  104.8 0.0 collective-permute-done.2
  104.8 0.4 concatenate
  105.3 0.7 constant_dynamic-slice_fusion.source
  106.0 1.8 %unfold.1 = bf16[16,4096]{1,0:T(8,128)(2,1)} custom-call(bf16[15,4608]{1,0:T(8,128)(2,1)} %constant_dynamic-slice_fusion.source), custom_call_target="tpu_custom_call" | custom-call | tf_op jit(solution)/shard_map/unfold/pallas_call | solution.py:226
  (1 shorter events, 0.0 us)
Async XLA Ops:
  4.0 37.9 %collective-permute-start = (bf16[1792,4096]{1,0:T(8,128)(2,1)}, bf16[1792,4096]{1,0:T(8,128)(2,1)S(1)}, u32[]{:S(2)}, u32[]{:S(2)}) collective-permute-start(bf16[1792,4096]{1,0:T(8,128)(2,1)} %param.9), channel_id=1, source_target_pairs={{0,1},{1,0},{2,3},{3,2},{4,5},{5,4},{6,7},{7,6},{8,9},{9,8},{10,11... | collective-permute-start | bytes 44040200 | tf_op jit(solution)/shard_map/ppermute | solution.py:244
  41.9 31.9 %collective-permute-start.1 = (bf16[1792,4096]{1,0:T(8,128)(2,1)S(1)}, bf16[1792,4096]{1,0:T(8,128)(2,1)S(1)}, u32[]{:S(2)}, u32[]{:S(2)}) collective-permute-start(bf16[1792,4096]{1,0:T(8,128)(2,1)S(1)} %collective-permute-done.other), channel_id=1, source_target_pairs={{0,1},{1,0},{2,3},{3,2},{4,5},{5,4},{6,7},{7,6},{8,9},{9,8},{10,11... | collective-permute-start | bytes 44040200 | tf_op jit(solution)/shard_map/ppermute | solution.py:248
  99.8 5.1 %collective-permute-start.2 = (bf16[7,4608]{1,0:T(8,128)(2,1)S(1)}, bf16[7,4608]{1,0:T(8,128)(2,1)S(1)}, u32[]{:S(2)}, u32[]{:S(2)}) collective-permute-start(bf16[7,4608]{1,0:T(8,128)(2,1)S(1)} %slice), channel_id=1, source_target_pairs={{0,2},{2,4},{4,6},{6,8},{8,10},{10,12},{12,14},{1,3},{3,5},{5,7},{... | collective-permute-start | bytes 193544

commit v5 on v4

--- a/solution.py
+++ b/solution.py
@@ -140,6 +140,7 @@
         out_specs=pl.BlockSpec(memory_space=pltpu.VMEM),
         out_shape=jax.ShapeDtypeStruct((devices // 2, 2, tokens, width), jnp.bfloat16),
         compiler_params=pltpu.CompilerParams(vmem_limit_bytes=20 << 20),
+        cost_estimate=pl.CostEstimate(flops=8_000_000_000, transcendentals=0, bytes_accessed=4_000_000),
         name="across_transform",
     )(source)
 
@@ -209,16 +210,10 @@
 
 def unfold_kernel(source, out):
     columns = out.shape[1]
-    shape = (out.shape[0], KEPT)
-    straight = picks(iota(shape, 0) == iota(shape, 1))
+    out[:KEPT, :] = source[:, :columns]
     extra = source[:, columns:]
     for piece in range(columns // COLUMNS):
-        lanes = pl.ds(piece * COLUMNS, COLUMNS)
-        last = picks((iota(shape, 0) == KEPT) & (iota(shape, 1) == piece))
-        out[:, lanes] = (
-            jnp.dot(straight, source[:, lanes], preferred_element_type=jnp.float32)
-            + jnp.dot(last, extra, preferred_element_type=jnp.float32)
-        ).astype(jnp.bfloat16)
+        out[KEPT:, pl.ds(piece * COLUMNS, COLUMNS)] = extra[piece : piece + 1]
 
 
 def unfold(source, tokens):
@@ -244,10 +239,8 @@
     other_weight = lax.ppermute(down_weight, "tensor", pairs)
     gathered = lax.all_to_all(inner.reshape(parts, own, width), "tensor", 0, 0)
     rotated = across_transform(gathered)
-    rotated, other_weight = lax.optimization_barrier((rotated, other_weight))
-    own_weight = lax.ppermute(other_weight, "tensor", pairs)
     back = lax.all_to_all(rotated, "tensor", 0, 0, axis_index_groups=same_core)
-    terms = product(back, other_weight, own_weight)
+    terms = product(back, other_weight, down_weight)
     total = lax.psum_scatter(
         terms, "tensor", scatter_dimension=0, axis_index_groups=same_core, tiled=True
     )

time: 108 us -> 107 us (level)
  starting transfers between devices: 8.2 us -> 5.98 us
  blocking collectives: 85.4 us -> 86.7 us
    ppermute x1 -> x0, starting transfers between devices: 3.16 us -> none  [per_device(): own_weight = lax.ppermute(other_weight, 'tensor', pairs)]
    all_to_all x1, blocking collectives: 28.8 us -> 30.5 us  [per_device(): back = lax.all_to_all(rotated, 'tensor', 0, 0, axis_index_groups=same_core)]
    unnamed x4 -> x12, local copies, waits for them, and re-layouts: 2.39 us -> 2.41 us
  transfers between devices with their start and end apart: 3 -> 2, of which waited for: 0 -> 0; matrix products, arithmetic and copies ran while one was open for 1% -> 1% of each run, Pallas kernels for 1% -> 1%
where the time goes in v5:
time: 107 us
  blocking collectives  86.7 us (81%)
  Pallas kernels  10.8 us (10%)
  starting transfers between devices  5.98 us (6%)
  local copies, waits for them, and re-layouts  2.41 us (2%)
    all_to_all x1, blocking collectives, per_device(): gathered = lax.all_to_all(inner.reshape(parts, own, width), 'tensor', 0, 0)  35.5 us
    all_to_all x1, blocking collectives, per_device(): back = lax.all_to_all(rotated, 'tensor', 0, 0, axis_index_groups=same_core)  30.5 us
    unnamed x1, blocking collectives  20.7 us
    pallas_call x1, Pallas kernels, product(): pl.pallas_call(product_kernel, in_specs=[vmem, vmem, vmem], out_specs=vme...  4.46 us
    unnamed x1, starting transfers between devices  4.05 us
    pallas_call x1, Pallas kernels, local_transform(): pl.pallas_call(local_kernel, in_specs=[pl.BlockSpec(memory_space=pl.ANY)]...  4.03 us
    unnamed x12, local copies, waits for them, and re-layouts  2.41 us
  transfers between devices with their start and end apart: 2, of which 0 were waited for; matrix products, arithmetic and copies ran while one was open for 1% of the time, Pallas kernels for 1%

profile of v5, /device:TPU:6, one launch (start us, length us, event | category | flops | bytes accessed | tf_op | source)
XLA Modules:
  0.0 106.6 jit_solution(5891343141467317680)
XLA Ops:
  0.0 4.0 %local_transform.1 = bf16[256,1792]{1,0:T(8,128)(2,1)S(1)} custom-call(bf16[256,1792]{1,0:T(8,128)(2,1)} %gate_hbm.1, bf16[256,1792]{1,0:T(8,128)(2,1)} %up_hbm.1, s32[1792]{0:T(1024)} %signs_hbm.1, s32[28,28]{1,0:T(8,128)} %hadamard_hbm.1), custom_call_target="tpu_custom_call" | custom-call | tf_op jit(solution)/shard_map/local_transform/pallas_call | solution.py:91
  4.0 1.9 %collective-permute-start = (bf16[1792,4096]{1,0:T(8,128)(2,1)}, bf16[1792,4096]{1,0:T(8,128)(2,1)S(1)}, u32[]{:S(2)}, u32[]{:S(2)}) collective-permute-start(bf16[1792,4096]{1,0:T(8,128)(2,1)} %own), channel_id=1, source_target_pairs={{0,1},{1,0},{2,3},{3,2},{4,5},{5,4},{6,7},{7,6},{8,9},{9,8},{10,11... | collective-permute-start | bytes 44040200 | tf_op jit(solution)/shard_map/ppermute | solution.py:239
  6.0 0.0 slice-start
  6.0 35.5 %all_to_all.10.source = bf16[16,16,1792]{2,1,0:T(8,128)(2,1)S(1)} all-to-all(bf16[16,16,1792]{2,1,0:T(8,128)(2,1)S(1)} %bitcast.6), channel_id=1, replica_groups=mesh['dp'=32,'tensor'=16] {'tensor'}, dimensions={0} | all-to-all | bytes 1835008 | tf_op jit(solution)/shard_map/all_to_all | solution.py:240
  41.5 0.0 slice-start.1
  41.5 0.0 slice-start.2
  41.5 0.0 slice-start.3
  41.5 0.7 across_transform.1
  42.2 30.5 %all_to_all.11.rows = bf16[8,2,16,1792]{3,2,1,0:T(8,128)(2,1)S(1)} all-to-all(bf16[8,2,16,1792]{3,2,1,0:T(8,128)(2,1)S(1)} %across_transform.1), channel_id=1, replica_groups={{0,2,4,6,8,10,12,14},{1,3,5,7,9,11,13,15},{16,18,20,22,24,26,28,30},{17..., dimensions={0} | all-to-all | bytes 1835008 | tf_op jit(solution)/shard_map/all_to_all | solution.py:242
  72.7 0.0 collective-permute-done.other
  72.7 0.0 slice-done
  72.7 0.0 slice-done.1
  72.7 0.0 slice-done.2
  72.7 0.0 slice-done.3
  72.8 4.5 %product.1 = bf16[120,4608]{1,0:T(8,128)(2,1)S(1)} custom-call(bf16[8,2,16,1792]{3,2,1,0:T(8,128)(2,1)S(1)} %all_to_all.11.rows, bf16[1792,4096]{1,0:T(8,128)(2,1)S(1)} %collective-permute-done.other, bf16[1792,4096]{1,0:T(8,128)(2,1)S(1)} %bitcast.5), custom_call_target="tpu_custom_call" | custom-call | flops 3758096384 | bytes 14680064 | tf_op jit(solution)/shard_map/product/pallas_call | solution.py:188
  77.2 20.7 %fusion = bf16[16,4608]{1,0:T(8,128)(2,1)S(1)} fusion(bf16[120,4608]{1,0:T(8,128)(2,1)S(1)} %product.1), kind=kCustom, calls=%all-reduce-scatter | all-reduce-scatter fusion | flops 589825 | bytes 1255424
  97.9 4.1 %collective-permute-start.1 = (bf16[7,4608]{1,0:T(8,128)(2,1)S(1)}, bf16[7,4608]{1,0:T(8,128)(2,1)S(1)}, u32[]{:S(2)}, u32[]{:S(2)}) collective-permute-start(bf16[7,4608]{1,0:T(8,128)(2,1)S(1)} %slice), channel_id=1, source_target_pairs={{0,2},{2,4},{4,6},{6,8},{8,10},{10,12},{12,14},{1,3},{3,5},{5,7},{... | collective-permute-start | bytes 193544
  102.0 1.3 %dynamic-slice.4 = u32[1]{0:T(128)} dynamic-slice(u32[512]{0:T(512)} %constant.2, u32[]{:S(6)} %partition-id.4), dynamic_slice_sizes={1} | dynamic-slice | bytes 12
  103.9 0.0 collective-permute-done.1
  103.9 0.4 concatenate
  104.4 0.7 constant_dynamic-slice_fusion.source
  105.1 1.6 %unfold.1 = bf16[16,4096]{1,0:T(8,128)(2,1)} custom-call(bf16[15,4608]{1,0:T(8,128)(2,1)} %constant_dynamic-slice_fusion.source), custom_call_target="tpu_custom_call" | custom-call | tf_op jit(solution)/shard_map/unfold/pallas_call | solution.py:221
  (2 shorter events, 0.0 us)
Async XLA Ops:
  4.0 68.7 %collective-permute-start = (bf16[1792,4096]{1,0:T(8,128)(2,1)}, bf16[1792,4096]{1,0:T(8,128)(2,1)S(1)}, u32[]{:S(2)}, u32[]{:S(2)}) collective-permute-start(bf16[1792,4096]{1,0:T(8,128)(2,1)} %own), channel_id=1, source_target_pairs={{0,1},{1,0},{2,3},{3,2},{4,5},{5,4},{6,7},{7,6},{8,9},{9,8},{10,11... | collective-permute-start | bytes 44040200 | tf_op jit(solution)/shard_map/ppermute | solution.py:239
  6.0 66.8 %slice-start = ((s8[14680064]{0:T(1024)(128)(4,1)}), s8[4194304]{0:T(1024)(128)(4,1)S(1)}, s32[]{:S(2)}) async-start(s8[14680064]{0:T(1024)(128)(4,1)} %bitcast.4), calls=%async_computation.2 | async-start | bytes 8388608
  41.5 31.2 %slice-start.1 = ((s8[14680064]{0:T(1024)(128)(4,1)}), s8[4194304]{0:T(1024)(128)(4,1)S(1)}, s32[]{:S(2)}) async-start(s8[14680064]{0:T(1024)(128)(4,1)} %bitcast.4), calls=%async_computation.3 | async-start | bytes 8388608
  41.5 31.2 %slice-start.2 = ((s8[14680064]{0:T(1024)(128)(4,1)}), s8[4194304]{0:T(1024)(128)(4,1)S(1)}, s32[]{:S(2)}) async-start(s8[14680064]{0:T(1024)(128)(4,1)} %bitcast.4), calls=%async_computation.4 | async-start | bytes 8388608
  41.5 31.3 %slice-start.3 = ((s8[14680064]{0:T(1024)(128)(4,1)}), s8[2097152]{0:T(1024)(128)(4,1)S(1)}, s32[]{:S(2)}) async-start(s8[14680064]{0:T(1024)(128)(4,1)} %bitcast.4), calls=%async_computation.5 | async-start | bytes 4194304
  97.9 6.0 %collective-permute-start.1 = (bf16[7,4608]{1,0:T(8,128)(2,1)S(1)}, bf16[7,4608]{1,0:T(8,128)(2,1)S(1)}, u32[]{:S(2)}, u32[]{:S(2)}) collective-permute-start(bf16[7,4608]{1,0:T(8,128)(2,1)S(1)} %slice), channel_id=1, source_target_pairs={{0,2},{2,4},{4,6},{6,8},{8,10},{10,12},{12,14},{1,3},{3,5},{5,7},{... | collective-permute-start | bytes 193544

commit v6 on v5

--- a/solution.py
+++ b/solution.py
@@ -29,25 +29,31 @@
     return jnp.where(condition, 1.0, 0.0).astype(jnp.bfloat16)
 
 
-def slab_matrix(hadamard):
+def outer_matrix():
     tall, wide = (SLAB, INNER), (INNER, SLAB)
-    tall_unit, wide_unit = iota(tall, 0), iota(wide, 1)
-    tall_outer, wide_outer = outer_index(tall_unit), outer_index(wide_unit)
-    pick_outer = picks(wide_outer == iota(wide, 0))
-    pick_inner = picks(wide_unit - ORDER * wide_outer == iota(wide, 0))[:ORDER]
-    tall_inner = picks(tall_unit - ORDER * tall_outer == iota(tall, 1))[:, :ORDER]
-    common = tall_outer & iota(tall, 1)
+    common = outer_index(iota(tall, 0)) & iota(tall, 1)
     for shift in (4, 2, 1):
         common = common ^ (common >> shift)
-    outer_rows = (1 - 2 * (common & 1)).astype(jnp.float32).astype(jnp.bfloat16)
-    inner_rows = jnp.dot(
-        tall_inner,
+    rows = (1 - 2 * (common & 1)).astype(jnp.float32).astype(jnp.bfloat16)
+    pick = picks(outer_index(iota(wide, 1)) == iota(wide, 0))
+    return jnp.dot(rows, pick, preferred_element_type=jnp.float32).astype(jnp.bfloat16)
+
+
+def inner_picks():
+    tall, wide = iota((SLAB, ORDER), 0), iota((ORDER, SLAB), 1)
+    return (
+        picks(tall - ORDER * outer_index(tall) == iota((SLAB, ORDER), 1)),
+        picks(wide - ORDER * outer_index(wide) == iota((ORDER, SLAB), 0)),
+    )
+
+
+def inner_matrix(hadamard, tall_pick, wide_pick):
+    rows = jnp.dot(
+        tall_pick,
         hadamard.astype(jnp.float32).astype(jnp.bfloat16),
         preferred_element_type=jnp.float32,
-    ).astype(jnp.bfloat16)
-    inner = jnp.dot(inner_rows, pick_inner, preferred_element_type=jnp.float32)
-    outer = jnp.dot(outer_rows, pick_outer, preferred_element_type=jnp.float32)
-    return (inner * outer).astype(jnp.bfloat16)
+    )
+    return jnp.dot(rows.astype(jnp.bfloat16), wide_pick, preferred_element_type=jnp.float32)
 
 
 def local_kernel(
@@ -70,12 +76,16 @@
         for copy in pair:
             copy.start()
         copies.append(pair)
+    matrix[...] = outer_matrix()
+    tall_pick, wide_pick = inner_picks()
     for copy in small:
         copy.wait()
-    matrix[...] = slab_matrix(hadamard[...])
-    for slab, pair in enumerate(copies):
+    inner = inner_matrix(hadamard[...], tall_pick, wide_pick)
+    matrix[...] = inner.astype(jnp.bfloat16) * matrix[...]
+    for pair in copies:
         for copy in pair:
             copy.wait()
+    for slab in range(width // SLAB):
         lanes = pl.ds(slab * SLAB, SLAB)
         half = 0.5 * gate[:, lanes].astype(jnp.float32)
         sign = signs[lanes].astype(jnp.float32).reshape(1, SLAB)
@@ -140,7 +150,9 @@
         out_specs=pl.BlockSpec(memory_space=pltpu.VMEM),
         out_shape=jax.ShapeDtypeStruct((devices // 2, 2, tokens, width), jnp.bfloat16),
         compiler_params=pltpu.CompilerParams(vmem_limit_bytes=20 << 20),
-        cost_estimate=pl.CostEstimate(flops=8_000_000_000, transcendentals=0, bytes_accessed=4_000_000),
+        cost_estimate=pl.CostEstimate(
+            flops=4_000_000_000, transcendentals=0, bytes_accessed=4_000_000
+        ),
         name="across_transform",
     )(source)
 

time: 107 us -> 106 us (level)
    unnamed x12 -> x6, local copies, waits for them, and re-layouts: 2.41 us -> 2.39 us
where the time goes in v6:
time: 106 us
  blocking collectives  86.4 us (82%)
  Pallas kernels  10 us (9%)
  starting transfers between devices  5.97 us (6%)
  local copies, waits for them, and re-layouts  2.39 us (2%)
    all_to_all x1, blocking collectives, per_device(): gathered = lax.all_to_all(inner.reshape(parts, own, width), 'tensor', 0, 0)  35.2 us
    all_to_all x1, blocking collectives, per_device(): back = lax.all_to_all(rotated, 'tensor', 0, 0, axis_index_groups=same_core)  30.5 us
    unnamed x1, blocking collectives  20.7 us
    pallas_call x1, Pallas kernels, product(): pl.pallas_call(product_kernel, in_specs=[vmem, vmem, vmem], out_specs=vme...  4.46 us
    unnamed x1, starting transfers between devices  4.05 us
    pallas_call x1, Pallas kernels, local_transform(): pl.pallas_call(local_kernel, in_specs=[pl.BlockSpec(memory_space=pl.ANY)]...  3.3 us
    unnamed x6, local copies, waits for them, and re-layouts  2.39 us
  transfers between devices with their start and end apart: 2, of which 0 were waited for; matrix products, arithmetic and copies ran while one was open for 1% of the time, Pallas kernels for 1%

profile of v6, /device:TPU:6, one launch (start us, length us, event | category | flops | bytes accessed | tf_op | source)
XLA Modules:
  0.0 105.6 jit_solution(7209083119299491197)
XLA Ops:
  0.0 3.3 %local_transform.1 = bf16[256,1792]{1,0:T(8,128)(2,1)S(1)} custom-call(bf16[256,1792]{1,0:T(8,128)(2,1)} %gate_hbm.1, bf16[256,1792]{1,0:T(8,128)(2,1)} %up_hbm.1, s32[1792]{0:T(1024)} %signs_hbm.1, s32[28,28]{1,0:T(8,128)} %hadamard_hbm.1), custom_call_target="tpu_custom_call" | custom-call | tf_op jit(solution)/shard_map/local_transform/pallas_call | solution.py:101
  3.3 1.9 %collective-permute-start = (bf16[1792,4096]{1,0:T(8,128)(2,1)}, bf16[1792,4096]{1,0:T(8,128)(2,1)S(1)}, u32[]{:S(2)}, u32[]{:S(2)}) collective-permute-start(bf16[1792,4096]{1,0:T(8,128)(2,1)} %own), channel_id=1, source_target_pairs={{0,1},{1,0},{2,3},{3,2},{4,5},{5,4},{6,7},{7,6},{8,9},{9,8},{10,11... | collective-permute-start | bytes 44040200 | tf_op jit(solution)/shard_map/ppermute | solution.py:251
  5.2 35.2 %all_to_all.10.source = bf16[16,16,1792]{2,1,0:T(8,128)(2,1)S(1)} all-to-all(bf16[16,16,1792]{2,1,0:T(8,128)(2,1)S(1)} %bitcast.4), channel_id=1, replica_groups=mesh['dp'=32,'tensor'=16] {'tensor'}, dimensions={0} | all-to-all | bytes 1835008 | tf_op jit(solution)/shard_map/all_to_all | solution.py:252
  40.5 0.0 copy-start
  40.5 0.7 across_transform.1
  41.2 30.5 %all_to_all.11.rows = bf16[8,2,16,1792]{3,2,1,0:T(8,128)(2,1)S(1)} all-to-all(bf16[8,2,16,1792]{3,2,1,0:T(8,128)(2,1)S(1)} %across_transform.1), channel_id=1, replica_groups={{0,2,4,6,8,10,12,14},{1,3,5,7,9,11,13,15},{16,18,20,22,24,26,28,30},{17..., dimensions={0} | all-to-all | bytes 1835008 | tf_op jit(solution)/shard_map/all_to_all | solution.py:254
  71.7 0.0 collective-permute-done.other
  71.7 0.0 copy-done
  71.7 4.5 %product.1 = bf16[120,4608]{1,0:T(8,128)(2,1)S(1)} custom-call(bf16[8,2,16,1792]{3,2,1,0:T(8,128)(2,1)S(1)} %all_to_all.11.rows, bf16[1792,4096]{1,0:T(8,128)(2,1)S(1)} %collective-permute-done.other, bf16[1792,4096]{1,0:T(8,128)(2,1)S(1)} %copy-done), custom_call_target="tpu_custom_call" | custom-call | flops 3758096384 | bytes 14680064 | tf_op jit(solution)/shard_map/product/pallas_call | solution.py:200
  76.2 20.7 %fusion = bf16[16,4608]{1,0:T(8,128)(2,1)S(1)} fusion(bf16[120,4608]{1,0:T(8,128)(2,1)S(1)} %product.1), kind=kCustom, calls=%all-reduce-scatter | all-reduce-scatter fusion | flops 589825 | bytes 1255424
  96.9 4.0 %collective-permute-start.1 = (bf16[7,4608]{1,0:T(8,128)(2,1)S(1)}, bf16[7,4608]{1,0:T(8,128)(2,1)S(1)}, u32[]{:S(2)}, u32[]{:S(2)}) collective-permute-start(bf16[7,4608]{1,0:T(8,128)(2,1)S(1)} %slice), channel_id=1, source_target_pairs={{0,2},{2,4},{4,6},{6,8},{8,10},{10,12},{12,14},{1,3},{3,5},{5,7},{... | collective-permute-start | bytes 193544
  100.9 1.3 %dynamic-slice.4 = u32[1]{0:T(128)} dynamic-slice(u32[512]{0:T(512)} %constant.2, u32[]{:S(6)} %partition-id.4), dynamic_slice_sizes={1} | dynamic-slice | bytes 12
  102.9 0.0 collective-permute-done.1
  102.9 0.4 concatenate
  103.3 0.7 constant_dynamic-slice_fusion.source
  104.0 1.6 %unfold.1 = bf16[16,4096]{1,0:T(8,128)(2,1)} custom-call(bf16[15,4608]{1,0:T(8,128)(2,1)} %constant_dynamic-slice_fusion.source), custom_call_target="tpu_custom_call" | custom-call | tf_op jit(solution)/shard_map/unfold/pallas_call | solution.py:233
  (1 shorter events, 0.0 us)
Async XLA Ops:
  3.3 68.4 %collective-permute-start = (bf16[1792,4096]{1,0:T(8,128)(2,1)}, bf16[1792,4096]{1,0:T(8,128)(2,1)S(1)}, u32[]{:S(2)}, u32[]{:S(2)}) collective-permute-start(bf16[1792,4096]{1,0:T(8,128)(2,1)} %own), channel_id=1, source_target_pairs={{0,1},{1,0},{2,3},{3,2},{4,5},{5,4},{6,7},{7,6},{8,9},{9,8},{10,11... | collective-permute-start | bytes 44040200 | tf_op jit(solution)/shard_map/ppermute | solution.py:251
  40.5 31.2 %copy-start = (bf16[1792,4096]{1,0:T(8,128)(2,1)S(1)}, bf16[1792,4096]{1,0:T(8,128)(2,1)}, u32[]{:S(2)}) copy-start(bf16[1792,4096]{1,0:T(8,128)(2,1)} %own) | copy-start | bytes 44040196
  96.9 6.0 %collective-permute-start.1 = (bf16[7,4608]{1,0:T(8,128)(2,1)S(1)}, bf16[7,4608]{1,0:T(8,128)(2,1)S(1)}, u32[]{:S(2)}, u32[]{:S(2)}) collective-permute-start(bf16[7,4608]{1,0:T(8,128)(2,1)S(1)} %slice), channel_id=1, source_target_pairs={{0,2},{2,4},{4,6},{6,8},{8,10},{10,12},{12,14},{1,3},{3,5},{5,7},{... | collective-permute-start | bytes 193544

commit v7 on v6

--- a/solution.py
+++ b/solution.py
@@ -54,6 +54,10 @@
         preferred_element_type=jnp.float32,
     )
     return jnp.dot(rows.astype(jnp.bfloat16), wide_pick, preferred_element_type=jnp.float32)
+
+
+def exchange_order(parts):
+    return list(range(0, parts, 2)) + list(range(parts - 1, 0, -2))
 
 
 def local_kernel(
@@ -90,9 +94,13 @@
         half = 0.5 * gate[:, lanes].astype(jnp.float32)
         sign = signs[lanes].astype(jnp.float32).reshape(1, SLAB)
         hidden = (half + half * jnp.tanh(half)) * (up[:, lanes].astype(jnp.float32) * sign)
-        out[:, lanes] = jnp.dot(
+        result = jnp.dot(
             hidden.astype(jnp.bfloat16), matrix[...], preferred_element_type=jnp.float32
         ).astype(jnp.bfloat16)
+        parts = lax.axis_size("tensor")
+        own = gate.shape[0] // parts
+        for position, device in enumerate(exchange_order(parts)):
+            out[pl.ds(position * own, own), lanes] = result[device * own : (device + 1) * own]
 
 
 def local_transform(gate, up, signs, hadamard):
@@ -124,9 +132,10 @@
     for chunk in range(SLAB // LANES):
         values = []
         for device in range(devices):
+            position = exchange_order(devices).index(device)
             for slab in range(slabs):
                 lanes = pl.ds(slab * SLAB + chunk * LANES, LANES)
-                values.append(source[device, :, lanes].astype(jnp.float32))
+                values.append(source[position, :, lanes].astype(jnp.float32))
         step = 1
         while step < len(values):
             for low in range(len(values)):
@@ -139,7 +148,8 @@
             chip, side = divmod(device, 2)
             lanes = pl.ds(slab * SLAB + chunk * LANES, LANES)
             place = core if side == 0 else 1 - core
-            out[chip, place, :, lanes] = (value * (1.0 / math.sqrt(FFN_UNITS))).astype(jnp.bfloat16)
+            target = jnp.where(core == 0, chip, devices // 2 - 1 - chip)
+            out[target, place, :, lanes] = (value * (1.0 / math.sqrt(FFN_UNITS))).astype(jnp.bfloat16)
 
 
 def across_transform(source):
@@ -244,12 +254,15 @@
     tokens, width = gate_pre.shape
     own = tokens // parts
     chips = parts // 2
-    same_core = [[2 * chip + side for chip in range(chips)] for side in range(2)]
     pairs = [(source, source ^ 1) for source in range(parts)]
     inner = local_transform(gate_pre, up_pre, signs, hadamard)
     inner, down_weight = lax.optimization_barrier((inner, down_weight))
     other_weight = lax.ppermute(down_weight, "tensor", pairs)
-    gathered = lax.all_to_all(inner.reshape(parts, own, width), "tensor", 0, 0)
+    everyone = [exchange_order(parts)]
+    same_core = [everyone[0][:chips], everyone[0][chips:]]
+    gathered = lax.all_to_all(
+        inner.reshape(parts, own, width), "tensor", 0, 0, axis_index_groups=everyone
+    )
     rotated = across_transform(gathered)
     back = lax.all_to_all(rotated, "tensor", 0, 0, axis_index_groups=same_core)
     terms = product(back, other_weight, down_weight)

time: 106 us -> 104 us (0.981)
  starting transfers between devices: 5.97 us -> 3.22 us
  blocking collectives: 86.4 us -> 87.5 us
    unnamed x1, blocking collectives: 20.7 us -> 24.4 us
    unnamed x1, starting transfers between devices: 4.05 us -> 1.29 us
    all_to_all x1, blocking collectives: 35.2 us -> 33.9 us  [per_device(): lax.all_to_all(inner.reshape(parts, own, width), 'tensor', 0, 0, axis_ind...]
    all_to_all x1, blocking collectives: 30.5 us -> 29.2 us  [per_device(): back = lax.all_to_all(rotated, 'tensor', 0, 0, axis_index_groups=same_core)]
where the time goes in v7:
time: 104 us
  blocking collectives  87.5 us (84%)
  Pallas kernels  9.93 us (10%)
  starting transfers between devices  3.22 us (3%)
  local copies, waits for them, and re-layouts  2.39 us (2%)
    all_to_all x1, blocking collectives, per_device(): lax.all_to_all(inner.reshape(parts, own, width), 'tensor', 0, 0, axis_ind...  33.9 us
    all_to_all x1, blocking collectives, per_device(): back = lax.all_to_all(rotated, 'tensor', 0, 0, axis_index_groups=same_core)  29.2 us
    unnamed x1, blocking collectives  24.4 us
    pallas_call x1, Pallas kernels, product(): pl.pallas_call(product_kernel, in_specs=[vmem, vmem, vmem], out_specs=vme...  4.46 us
    pallas_call x1, Pallas kernels, local_transform(): pl.pallas_call(local_kernel, in_specs=[pl.BlockSpec(memory_space=pl.ANY)]...  3.3 us
    unnamed x6, local copies, waits for them, and re-layouts  2.39 us
  transfers between devices with their start and end apart: 2, of which 0 were waited for; matrix products, arithmetic and copies ran while one was open for 1% of the time, Pallas kernels for 1%

profile of v7, /device:TPU:6, one launch (start us, length us, event | category | flops | bytes accessed | tf_op | source)
XLA Modules:
  0.0 103.8 jit_solution(12994790679766474930)
XLA Ops:
  0.0 3.3 %local_transform.1 = bf16[256,1792]{1,0:T(8,128)(2,1)S(1)} custom-call(bf16[256,1792]{1,0:T(8,128)(2,1)} %gate_hbm.1, bf16[256,1792]{1,0:T(8,128)(2,1)} %up_hbm.1, s32[1792]{0:T(1024)} %signs_hbm.1, s32[28,28]{1,0:T(8,128)} %hadamard_hbm.1), custom_call_target="tpu_custom_call" | custom-call | tf_op jit(solution)/shard_map/local_transform/pallas_call | solution.py:109
  3.3 1.9 %collective-permute-start = (bf16[1792,4096]{1,0:T(8,128)(2,1)}, bf16[1792,4096]{1,0:T(8,128)(2,1)S(1)}, u32[]{:S(2)}, u32[]{:S(2)}) collective-permute-start(bf16[1792,4096]{1,0:T(8,128)(2,1)} %own), channel_id=1, source_target_pairs={{0,1},{1,0},{2,3},{3,2},{4,5},{5,4},{6,7},{7,6},{8,9},{9,8},{10,11... | collective-permute-start | bytes 44040200 | tf_op jit(solution)/shard_map/ppermute | solution.py:260
  5.2 33.9 %all_to_all.10.source = bf16[16,16,1792]{2,1,0:T(8,128)(2,1)S(1)} all-to-all(bf16[16,16,1792]{2,1,0:T(8,128)(2,1)S(1)} %bitcast.4), channel_id=1, replica_groups={{0,2,4,6,8,10,12,14,15,13,11,9,7,5,3,1},{16,18,20,22,24,26,28,30,31,29,..., dimensions={0} | all-to-all | bytes 1835008 | tf_op jit(solution)/shard_map/all_to_all | solution.py:263
  39.1 0.0 copy-start
  39.1 0.6 across_transform.1
  39.7 29.2 %all_to_all.11.rows = bf16[8,2,16,1792]{3,2,1,0:T(8,128)(2,1)S(1)} all-to-all(bf16[8,2,16,1792]{3,2,1,0:T(8,128)(2,1)S(1)} %across_transform.1), channel_id=1, replica_groups={{0,2,4,6,8,10,12,14},{15,13,11,9,7,5,3,1},{16,18,20,22,24,26,28,30},{31..., dimensions={0} | all-to-all | bytes 1835008 | tf_op jit(solution)/shard_map/all_to_all | solution.py:267
  69.0 0.0 collective-permute-done.other
  69.0 0.0 copy-done
  69.0 4.5 %product.1 = bf16[120,4608]{1,0:T(8,128)(2,1)S(1)} custom-call(bf16[8,2,16,1792]{3,2,1,0:T(8,128)(2,1)S(1)} %all_to_all.11.rows, bf16[1792,4096]{1,0:T(8,128)(2,1)S(1)} %collective-permute-done.other, bf16[1792,4096]{1,0:T(8,128)(2,1)S(1)} %copy-done), custom_call_target="tpu_custom_call" | custom-call | flops 3758096384 | bytes 14680064 | tf_op jit(solution)/shard_map/product/pallas_call | solution.py:210
  73.4 24.4 %fusion = bf16[16,4608]{1,0:T(8,128)(2,1)S(1)} fusion(bf16[120,4608]{1,0:T(8,128)(2,1)S(1)} %product.1), kind=kCustom, calls=%all-reduce-scatter | all-reduce-scatter fusion | flops 589825 | bytes 1255424
  97.9 1.3 %collective-permute-start.1 = (bf16[7,4608]{1,0:T(8,128)(2,1)S(1)}, bf16[7,4608]{1,0:T(8,128)(2,1)S(1)}, u32[]{:S(2)}, u32[]{:S(2)}) collective-permute-start(bf16[7,4608]{1,0:T(8,128)(2,1)S(1)} %slice), channel_id=1, source_target_pairs={{0,2},{2,4},{4,6},{6,8},{8,10},{10,12},{12,14},{15,13},{13,11},{11... | collective-permute-start | bytes 193544
  99.2 1.3 %dynamic-slice.4 = u32[1]{0:T(128)} dynamic-slice(u32[512]{0:T(512)} %constant.2, u32[]{:S(6)} %partition-id.4), dynamic_slice_sizes={1} | dynamic-slice | bytes 12
  101.1 0.0 collective-permute-done.1
  101.1 0.4 concatenate
  101.5 0.7 constant_dynamic-slice_fusion.source
  102.2 1.6 %unfold.1 = bf16[16,4096]{1,0:T(8,128)(2,1)} custom-call(bf16[15,4608]{1,0:T(8,128)(2,1)} %constant_dynamic-slice_fusion.source), custom_call_target="tpu_custom_call" | custom-call | tf_op jit(solution)/shard_map/unfold/pallas_call | solution.py:243
  (1 shorter events, 0.0 us)
Async XLA Ops:
  3.3 65.7 %collective-permute-start = (bf16[1792,4096]{1,0:T(8,128)(2,1)}, bf16[1792,4096]{1,0:T(8,128)(2,1)S(1)}, u32[]{:S(2)}, u32[]{:S(2)}) collective-permute-start(bf16[1792,4096]{1,0:T(8,128)(2,1)} %own), channel_id=1, source_target_pairs={{0,1},{1,0},{2,3},{3,2},{4,5},{5,4},{6,7},{7,6},{8,9},{9,8},{10,11... | collective-permute-start | bytes 44040200 | tf_op jit(solution)/shard_map/ppermute | solution.py:260
  39.1 29.8 %copy-start = (bf16[1792,4096]{1,0:T(8,128)(2,1)S(1)}, bf16[1792,4096]{1,0:T(8,128)(2,1)}, u32[]{:S(2)}) copy-start(bf16[1792,4096]{1,0:T(8,128)(2,1)} %own) | copy-start | bytes 44040196
  97.9 3.3 %collective-permute-start.1 = (bf16[7,4608]{1,0:T(8,128)(2,1)S(1)}, bf16[7,4608]{1,0:T(8,128)(2,1)S(1)}, u32[]{:S(2)}, u32[]{:S(2)}) collective-permute-start(bf16[7,4608]{1,0:T(8,128)(2,1)S(1)} %slice), channel_id=1, source_target_pairs={{0,2},{2,4},{4,6},{6,8},{8,10},{10,12},{12,14},{15,13},{13,11},{11... | collective-permute-start | bytes 193544

commit v8 on v7

--- a/solution.py
+++ b/solution.py
@@ -232,10 +232,16 @@
 
 def unfold_kernel(source, out):
     columns = out.shape[1]
-    out[:KEPT, :] = source[:, :columns]
+    shape = (out.shape[0], KEPT)
+    straight = picks(iota(shape, 0) == iota(shape, 1))
     extra = source[:, columns:]
     for piece in range(columns // COLUMNS):
-        out[KEPT:, pl.ds(piece * COLUMNS, COLUMNS)] = extra[piece : piece + 1]
+        lanes = pl.ds(piece * COLUMNS, COLUMNS)
+        last = picks((iota(shape, 0) == KEPT) & (iota(shape, 1) == piece))
+        out[:, lanes] = (
+            jnp.dot(straight, source[:, lanes], preferred_element_type=jnp.float32)
+            + jnp.dot(last, extra, preferred_element_type=jnp.float32)
+        ).astype(jnp.bfloat16)
 
 
 def unfold(source, tokens):

time: 104 us -> 104 us (level)
  no operation moved by 1% of the time
where the time goes in v8:
time: 104 us
  blocking collectives  87.5 us (84%)
  Pallas kernels  10.1 us (10%)
  starting transfers between devices  3.22 us (3%)
  local copies, waits for them, and re-layouts  2.39 us (2%)
    all_to_all x1, blocking collectives, per_device(): lax.all_to_all(inner.reshape(parts, own, width), 'tensor', 0, 0, axis_ind...  33.9 us
    all_to_all x1, blocking collectives, per_device(): back = lax.all_to_all(rotated, 'tensor', 0, 0, axis_index_groups=same_core)  29.2 us
    unnamed x1, blocking collectives  24.4 us
    pallas_call x1, Pallas kernels, product(): pl.pallas_call(product_kernel, in_specs=[vmem, vmem, vmem], out_specs=vme...  4.46 us
    pallas_call x1, Pallas kernels, local_transform(): pl.pallas_call(local_kernel, in_specs=[pl.BlockSpec(memory_space=pl.ANY)]...  3.3 us
    unnamed x6, local copies, waits for them, and re-layouts  2.39 us
  transfers between devices with their start and end apart: 2, of which 0 were waited for; matrix products, arithmetic and copies ran while one was open for 1% of the time, Pallas kernels for 1%

profile of v8, /device:TPU:6, one launch (start us, length us, event | category | flops | bytes accessed | tf_op | source)
XLA Modules:
  0.0 104.0 jit_solution(9428168869735414155)
XLA Ops:
  0.0 3.3 %local_transform.1 = bf16[256,1792]{1,0:T(8,128)(2,1)S(1)} custom-call(bf16[256,1792]{1,0:T(8,128)(2,1)} %gate_hbm.1, bf16[256,1792]{1,0:T(8,128)(2,1)} %up_hbm.1, s32[1792]{0:T(1024)} %signs_hbm.1, s32[28,28]{1,0:T(8,128)} %hadamard_hbm.1), custom_call_target="tpu_custom_call" | custom-call | tf_op jit(solution)/shard_map/local_transform/pallas_call | solution.py:109
  3.3 1.9 %collective-permute-start = (bf16[1792,4096]{1,0:T(8,128)(2,1)}, bf16[1792,4096]{1,0:T(8,128)(2,1)S(1)}, u32[]{:S(2)}, u32[]{:S(2)}) collective-permute-start(bf16[1792,4096]{1,0:T(8,128)(2,1)} %own), channel_id=1, source_target_pairs={{0,1},{1,0},{2,3},{3,2},{4,5},{5,4},{6,7},{7,6},{8,9},{9,8},{10,11... | collective-permute-start | bytes 44040200 | tf_op jit(solution)/shard_map/ppermute | solution.py:266
  5.2 33.9 %all_to_all.10.source = bf16[16,16,1792]{2,1,0:T(8,128)(2,1)S(1)} all-to-all(bf16[16,16,1792]{2,1,0:T(8,128)(2,1)S(1)} %bitcast.4), channel_id=1, replica_groups={{0,2,4,6,8,10,12,14,15,13,11,9,7,5,3,1},{16,18,20,22,24,26,28,30,31,29,..., dimensions={0} | all-to-all | bytes 1835008 | tf_op jit(solution)/shard_map/all_to_all | solution.py:269
  39.1 0.0 copy-start
  39.1 0.6 across_transform.1
  39.7 29.2 %all_to_all.11.rows = bf16[8,2,16,1792]{3,2,1,0:T(8,128)(2,1)S(1)} all-to-all(bf16[8,2,16,1792]{3,2,1,0:T(8,128)(2,1)S(1)} %across_transform.1), channel_id=1, replica_groups={{0,2,4,6,8,10,12,14},{15,13,11,9,7,5,3,1},{16,18,20,22,24,26,28,30},{31..., dimensions={0} | all-to-all | bytes 1835008 | tf_op jit(solution)/shard_map/all_to_all | solution.py:273
  69.0 0.0 collective-permute-done.other
  69.0 0.0 copy-done
  69.0 4.5 %product.1 = bf16[120,4608]{1,0:T(8,128)(2,1)S(1)} custom-call(bf16[8,2,16,1792]{3,2,1,0:T(8,128)(2,1)S(1)} %all_to_all.11.rows, bf16[1792,4096]{1,0:T(8,128)(2,1)S(1)} %collective-permute-done.other, bf16[1792,4096]{1,0:T(8,128)(2,1)S(1)} %copy-done), custom_call_target="tpu_custom_call" | custom-call | flops 3758096384 | bytes 14680064 | tf_op jit(solution)/shard_map/product/pallas_call | solution.py:210
  73.4 24.4 %fusion = bf16[16,4608]{1,0:T(8,128)(2,1)S(1)} fusion(bf16[120,4608]{1,0:T(8,128)(2,1)S(1)} %product.1), kind=kCustom, calls=%all-reduce-scatter | all-reduce-scatter fusion | flops 589825 | bytes 1255424
  97.9 1.3 %collective-permute-start.1 = (bf16[7,4608]{1,0:T(8,128)(2,1)S(1)}, bf16[7,4608]{1,0:T(8,128)(2,1)S(1)}, u32[]{:S(2)}, u32[]{:S(2)}) collective-permute-start(bf16[7,4608]{1,0:T(8,128)(2,1)S(1)} %slice), channel_id=1, source_target_pairs={{0,2},{2,4},{4,6},{6,8},{8,10},{10,12},{12,14},{15,13},{13,11},{11... | collective-permute-start | bytes 193544
  99.2 1.3 %dynamic-slice.4 = u32[1]{0:T(128)} dynamic-slice(u32[512]{0:T(512)} %constant.2, u32[]{:S(6)} %partition-id.4), dynamic_slice_sizes={1} | dynamic-slice | bytes 12
  101.1 0.0 collective-permute-done.1
  101.1 0.4 concatenate
  101.5 0.7 constant_dynamic-slice_fusion.source
  102.2 1.8 %unfold.1 = bf16[16,4096]{1,0:T(8,128)(2,1)} custom-call(bf16[15,4608]{1,0:T(8,128)(2,1)} %constant_dynamic-slice_fusion.source), custom_call_target="tpu_custom_call" | custom-call | tf_op jit(solution)/shard_map/unfold/pallas_call | solution.py:249
  (1 shorter events, 0.0 us)
Async XLA Ops:
  3.3 65.7 %collective-permute-start = (bf16[1792,4096]{1,0:T(8,128)(2,1)}, bf16[1792,4096]{1,0:T(8,128)(2,1)S(1)}, u32[]{:S(2)}, u32[]{:S(2)}) collective-permute-start(bf16[1792,4096]{1,0:T(8,128)(2,1)} %own), channel_id=1, source_target_pairs={{0,1},{1,0},{2,3},{3,2},{4,5},{5,4},{6,7},{7,6},{8,9},{9,8},{10,11... | collective-permute-start | bytes 44040200 | tf_op jit(solution)/shard_map/ppermute | solution.py:266
  39.1 29.8 %copy-start = (bf16[1792,4096]{1,0:T(8,128)(2,1)S(1)}, bf16[1792,4096]{1,0:T(8,128)(2,1)}, u32[]{:S(2)}) copy-start(bf16[1792,4096]{1,0:T(8,128)(2,1)} %own) | copy-start | bytes 44040196
  97.9 3.3 %collective-permute-start.1 = (bf16[7,4608]{1,0:T(8,128)(2,1)S(1)}, bf16[7,4608]{1,0:T(8,128)(2,1)S(1)}, u32[]{:S(2)}, u32[]{:S(2)}) collective-permute-start(bf16[7,4608]{1,0:T(8,128)(2,1)S(1)} %slice), channel_id=1, source_target_pairs={{0,2},{2,4},{4,6},{6,8},{8,10},{10,12},{12,14},{15,13},{13,11},{11... | collective-permute-start | bytes 193544
